TPU v7x, 32 devices: a whole 2x2x4 slice. The times are simulated.
32 devices in a mesh: grp: 2 (over x), lx: 4 (over y, core), ly: 4 (over z).
Axes of the slice: x: 2, y: 2, z: 4, core: 2. Of those that a mesh axis runs over, the one named last changes fastest.
Arguments:
- vectors: float32 [8, 256, 2048], P('grp', 'lx', 'ly'), may hold values from -6 to 6
- levels: int32 [256, 2048], P('lx', 'ly'), may hold values from 0 to 7
- level_table: float32 [8], replicated, may hold values from 1 to 3
- filter_low: float32 [1], replicated, may hold values from -1 to 0.5
- filter_high: float32 [1], replicated, may hold values from 6 to 7.5
Outputs:
- basis: float32 [8, 256, 2048], P('grp', 'lx', 'ly')
All inputs are finite; a program needn't handle non-finite values.
Results may differ from a plain program's by a relative error of at most 0.00011.
Values sent between devices are 32-bit elements; how exact they have to be, the bound alone decides.
A program may use at most 64 MiB of HBM per device.

v0:
```python
import jax
import jax.numpy as jnp
from jax import lax
from jax.sharding import PartitionSpec as P


def padded_2(shard, sides, width):
    for axis, dim in sides:
        size, length = (lax.axis_size(axis), shard.shape[dim])
        up = [(i, (i + 1) % size) for i in range(size)]
        down = [(j, i) for i, j in up]
        last = lax.slice_in_dim(shard, length - width, length, axis=dim)
        leading = lax.slice_in_dim(shard, 0, width, axis=dim)
        before = lax.ppermute(last, axis, up)
        after = lax.ppermute(leading, axis, down)
        shard = jnp.concatenate([before, shard, after], axis=dim)
    return shard


def from_root(value, axis, source):
    kept = jnp.where(lax.axis_index(axis) == source, value, 0).astype(value.dtype)
    return lax.psum(kept, axis)


def apply_operator(field, onsite):
    padded = padded_2(field, (("lx", 1), ("ly", 2)), 1)
    beside = padded[:, 2:, 1:-1] + padded[:, :-2, 1:-1] + padded[:, 1:-1, 2:] + padded[:, 1:-1, :-2]
    return onsite[None] * field - beside


def lower_inverse(gram):
    lower = jnp.linalg.cholesky(gram)
    eye_block = jnp.eye(gram.shape[0], dtype=jnp.float32)
    return lax.linalg.triangular_solve(lower, eye_block, left_side=True, lower=True)


def body(vectors, levels, level_table, filter_low, filter_high):
    count_vec, rows_local, cols_local = vectors.shape
    level_ids = jnp.arange(level_table.shape[0], dtype=jnp.int32)
    onsite = jnp.sum(
        jnp.where(levels[None] == level_ids[:, None, None], level_table[:, None, None], 0.0), axis=0
    )
    center = (filter_high[0] + filter_low[0]) / 2.0
    half = (filter_high[0] - filter_low[0]) / 2.0
    first = (apply_operator(vectors, onsite) - center * vectors) / half
    filtered = 2.0 * (apply_operator(first, onsite) - center * first) / half - vectors
    total = rows_local * cols_local * lax.axis_size("lx") * lax.axis_size("ly")
    flat = filtered.reshape(count_vec, rows_local * cols_local)
    highest = lax.Precision.HIGHEST
    mine = lax.axis_index("grp")
    result = jnp.zeros_like(flat)
    for h in range(lax.axis_size("grp")):
        gram = lax.psum(jnp.dot(flat, flat.T, precision=highest), ("lx", "ly")) / total
        done = jnp.dot(lower_inverse(gram), flat, precision=highest)
        result = jnp.where(mine == h, done, result)
        shared = from_root(done, "grp", h)
        coeff = lax.psum(jnp.dot(shared, flat.T, precision=highest), ("lx", "ly")) / total
        later = mine > h
        flat = jnp.where(later, flat - jnp.dot(coeff.T, shared, precision=highest), flat)
    return result.reshape(count_vec, rows_local, cols_local)


def solution(mesh):
    in_specs = (P("grp", "lx", "ly"), P("lx", "ly"), P(), P(), P())
    out_specs = P("grp", "lx", "ly")
    return jax.shard_map(body, mesh=mesh, in_specs=in_specs, out_specs=out_specs, check_vma=False)
```

profile of v0, /device:TPU:2, one launch (start us, length us, event | category | flops | bytes accessed | tf_op | source)
XLA Modules:
  0.0 183.2 jit_solution(6349266937736185000)
XLA Ops:
  6.5 0.9 fusion.32
  7.5 1.7 collective-permute-start
  9.2 1.3 collective-permute-done.1
  10.6 1.1 pad_maximum_fusion.21
  11.7 3.7 %collective-permute-start.2 = (f32[4,66,1]{2,1,0:T(8,128)S(1)}, f32[4,66,1]{2,1,0:T(8,128)S(1)}, u32[]{:S(2)}, u32[]{:S(2)}) collective-permute-start(f32[4,66,1]{2,1,0:T(8,128)S(1)} %get-tuple-element.9), channel_id=1, source_target_pairs={{1,0},{2,1},{3,2},{0,3},{5,4},{6,5},{7,6},{4,7},{9,8},{10,9},{11,1... | collective-permute-start | bytes 3176 | tf_op jit(solution)/shard_map/ppermute | solution.py:15
  16.8 2.2 %collective-permute-done.2 = f32[4,66,1]{2,1,0:T(8,128)S(1)} collective-permute-done((f32[4,66,1]{2,1,0:T(8,128)S(1)}, f32[4,66,1]{2,1,0:T(8,128)S(1)}, u32[]{:S(2)}, u32[]{:S(2)}) %collective-permute-start.2) | collective-permute-done | bytes 1088 | tf_op jit(solution)/shard_map/ppermute | solution.py:15
  19.1 4.6 %collective-permute-done.3 = f32[4,66,1]{2,1,0:T(8,128)S(1)} collective-permute-done((f32[4,66,1]{2,1,0:T(8,128)S(1)}, f32[4,66,1]{2,1,0:T(8,128)S(1)}, u32[]{:S(2)}, u32[]{:S(2)}) %collective-permute-start.3) | collective-permute-done | bytes 1088 | tf_op jit(solution)/shard_map/ppermute | solution.py:14
  24.2 1.6 collective-permute-start.4
  25.9 1.3 collective-permute-done.5
  27.4 1.9 %collective-permute-start.6 = (f32[4,66,1]{2,1,0:T(8,128)S(1)}, f32[4,66,1]{2,1,0:T(8,128)S(1)}, u32[]{:S(2)}, u32[]{:S(2)}) collective-permute-start(f32[4,66,1]{2,1,0:T(8,128)S(1)} %get-tuple-element.6), channel_id=1, source_target_pairs={{1,0},{2,1},{3,2},{0,3},{5,4},{6,5},{7,6},{4,7},{9,8},{10,9},{11,1... | collective-permute-start | bytes 3176 | tf_op jit(solution)/shard_map/ppermute | solution.py:15
  29.4 4.4 %collective-permute-done.6 = f32[4,66,1]{2,1,0:T(8,128)S(1)} collective-permute-done((f32[4,66,1]{2,1,0:T(8,128)S(1)}, f32[4,66,1]{2,1,0:T(8,128)S(1)}, u32[]{:S(2)}, u32[]{:S(2)}) %collective-permute-start.6) | collective-permute-done | bytes 1088 | tf_op jit(solution)/shard_map/ppermute | solution.py:15
  33.9 4.0 %collective-permute-done.7 = f32[4,66,1]{2,1,0:T(8,128)S(1)} collective-permute-done((f32[4,66,1]{2,1,0:T(8,128)S(1)}, f32[4,66,1]{2,1,0:T(8,128)S(1)}, u32[]{:S(2)}, u32[]{:S(2)}) %collective-permute-start.7) | collective-permute-done | bytes 1088 | tf_op jit(solution)/shard_map/ppermute | solution.py:14
  38.3 2.4 %convolution_bitcast_fusion = f32[4,4]{0,1:T(4,128)S(1)} fusion(f32[4,64,512]{2,1,0:T(8,128)S(1)} %fusion.6), kind=kOutput, calls=%fused_computation.4 | convolution fusion | flops 6291456 | bytes 524352 | tf_op jit(solution)/shard_map/dot_general | solution.py:53
  40.7 31.0 %psum.28 = f32[4,4]{0,1:T(4,128)S(1)} all-reduce(f32[4,4]{0,1:T(4,128)S(1)} %convolution_bitcast_fusion), channel_id=1, replica_groups=mesh['grp'=2,'lx'=4,'ly'=4] {'lx','ly'}, use_global_device_ids=true, to_apply=%region_1.2 | all-reduce | flops 16 | bytes 128 | tf_op jit(solution)/shard_map/psum | solution.py:53
  74.4 1.8 convolution_select_fusion.1
  76.2 25.6 %all-reduce.2.cloned.1.call-done = f32[4,32768]{1,0:T(4,128)} async-done(((f32[4,32768]{1,0:T(4,128)}), f32[4,32768]{1,0:T(4,128)}) %all-reduce.2.cloned.1.call-update) | async-done | bytes 524304 | tf_op jit(solution)/shard_map/psum | solution.py:22
  101.8 3.5 %fusion.33 = f32[4,4]{0,1:T(4,128)S(1)} fusion(f32[4,32768]{1,0:T(4,128)} %all-reduce.2.cloned.1.call-done, f32[4,32768]{1,0:T(4,128)S(1)} %bitcast.40), kind=kOutput, calls=%fused_computation.73 | convolution fusion | flops 6291456 | bytes 1048640 | tf_op jit(solution)/shard_map/dot_general | solution.py:57
  105.3 33.6 %psum.30 = f32[4,4]{0,1:T(4,128)S(1)} all-reduce(f32[4,4]{0,1:T(4,128)S(1)} %fusion.33), channel_id=1, replica_groups=mesh['grp'=2,'lx'=4,'ly'=4] {'lx','ly'}, use_global_device_ids=true, to_apply=%region_5.8 | all-reduce | flops 16 | bytes 128 | tf_op jit(solution)/shard_map/psum | solution.py:57
  138.9 1.0 fusion
  139.9 2.3 %fusion.34 = f32[4,4]{0,1:T(4,128)S(1)} fusion(f32[4,32768]{1,0:T(4,128)S(1)} %fusion), kind=kOutput, calls=%fused_computation.74 | convolution fusion | flops 6291456 | bytes 524352 | tf_op jit(solution)/shard_map/dot_general | solution.py:53
  142.2 29.7 %psum.31 = f32[4,4]{0,1:T(4,128)S(1)} all-reduce(f32[4,4]{0,1:T(4,128)S(1)} %fusion.34), channel_id=1, replica_groups=mesh['grp'=2,'lx'=4,'ly'=4] {'lx','ly'}, use_global_device_ids=true, to_apply=%region_6.9 | all-reduce | flops 16 | bytes 128 | tf_op jit(solution)/shard_map/psum | solution.py:53
  172.4 0.7 compare_reduce_fusion
  174.4 1.0 convolution_select_fusion
  175.4 1.0 copy.30
  (41 shorter events, 6.1 us)
Async XLA Ops:
  6.5 95.2 %all-reduce.2.cloned.1.call-start = ((), (), s32[]{:S(2)}) async-start(), calls=%async_computation | async-start | bytes 1048576 | tf_op jit(solution)/shard_map/psum | solution.py:22
  7.4 3.1 %collective-permute-start.1 = (f32[4,1,512]{2,1,0:T(1,128)S(1)}, f32[4,1,512]{2,1,0:T(1,128)S(1)}, u32[]{:S(2)}, u32[]{:S(2)}) collective-permute-start(f32[4,1,512]{2,1,0:T(1,128)S(1)} %get-tuple-element.13), channel_id=1, source_target_pairs={{0,4},{4,8},{8,12},{12,0},{1,5},{5,9},{9,13},{13,1},{2,6},{6,10},{... | collective-permute-start | bytes 24584 | tf_op jit(solution)/shard_map/ppermute | solution.py:14
  7.5 7.9 %copy-start.3 = (s32[64,512]{1,0:T(8,128)S(1)}, s32[64,512]{1,0:T(8,128)}, u32[]{:S(2)}) copy-start(s32[64,512]{1,0:T(8,128)} %param.9) | copy-start | bytes 393220
  7.5 16.1 %copy-start = (f32[4,64,512]{2,1,0:T(8,128)S(1)}, f32[4,64,512]{2,1,0:T(8,128)}, u32[]{:S(2)}) copy-start(f32[4,64,512]{2,1,0:T(8,128)} %param.8) | copy-start | bytes 1572868
  7.5 3.1 %collective-permute-start = (f32[4,1,512]{2,1,0:T(1,128)S(1)}, f32[4,1,512]{2,1,0:T(1,128)S(1)}, u32[]{:S(2)}, u32[]{:S(2)}) collective-permute-start(f32[4,1,512]{2,1,0:T(1,128)S(1)} %get-tuple-element.14), channel_id=1, source_target_pairs={{4,0},{8,4},{12,8},{0,12},{5,1},{9,5},{13,9},{1,13},{6,2},{10,6},{... | collective-permute-start | bytes 24584 | tf_op jit(solution)/shard_map/ppermute | solution.py:15
  11.7 3.7 %copy-start.4 = (f32[8]{0:T(128)S(1)}, f32[8]{0:T(128)}, u32[]{:S(2)}) copy-start(f32[8]{0:T(128)} %param.10) | copy-start | bytes 100
  11.7 7.4 %collective-permute-start.2 = (f32[4,66,1]{2,1,0:T(8,128)S(1)}, f32[4,66,1]{2,1,0:T(8,128)S(1)}, u32[]{:S(2)}, u32[]{:S(2)}) collective-permute-start(f32[4,66,1]{2,1,0:T(8,128)S(1)} %get-tuple-element.9), channel_id=1, source_target_pairs={{1,0},{2,1},{3,2},{0,3},{5,4},{6,5},{7,6},{4,7},{9,8},{10,9},{11,1... | collective-permute-start | bytes 3176 | tf_op jit(solution)/shard_map/ppermute | solution.py:15
  15.4 8.3 %collective-permute-start.3 = (f32[4,66,1]{2,1,0:T(8,128)S(1)}, f32[4,66,1]{2,1,0:T(8,128)S(1)}, u32[]{:S(2)}, u32[]{:S(2)}) collective-permute-start(f32[4,66,1]{2,1,0:T(8,128)S(1)} %get-tuple-element.10), channel_id=1, source_target_pairs={{0,1},{1,2},{2,3},{3,0},{4,5},{5,6},{6,7},{7,4},{8,9},{9,10},{10,1... | collective-permute-start | bytes 3176 | tf_op jit(solution)/shard_map/ppermute | solution.py:14
  24.1 3.1 %collective-permute-start.5 = (f32[4,1,512]{2,1,0:T(1,128)S(1)}, f32[4,1,512]{2,1,0:T(1,128)S(1)}, u32[]{:S(2)}, u32[]{:S(2)}) collective-permute-start(f32[4,1,512]{2,1,0:T(1,128)S(1)} %get-tuple-element.11), channel_id=1, source_target_pairs={{0,4},{4,8},{8,12},{12,0},{1,5},{5,9},{9,13},{13,1},{2,6},{6,10},{... | collective-permute-start | bytes 24584 | tf_op jit(solution)/shard_map/ppermute | solution.py:14
  24.2 3.0 %collective-permute-start.4 = (f32[4,1,512]{2,1,0:T(1,128)S(1)}, f32[4,1,512]{2,1,0:T(1,128)S(1)}, u32[]{:S(2)}, u32[]{:S(2)}) collective-permute-start(f32[4,1,512]{2,1,0:T(1,128)S(1)} %get-tuple-element.12), channel_id=1, source_target_pairs={{4,0},{8,4},{12,8},{0,12},{5,1},{9,5},{13,9},{1,13},{6,2},{10,6},{... | collective-permute-start | bytes 24584 | tf_op jit(solution)/shard_map/ppermute | solution.py:15
  27.4 6.5 %collective-permute-start.6 = (f32[4,66,1]{2,1,0:T(8,128)S(1)}, f32[4,66,1]{2,1,0:T(8,128)S(1)}, u32[]{:S(2)}, u32[]{:S(2)}) collective-permute-start(f32[4,66,1]{2,1,0:T(8,128)S(1)} %get-tuple-element.6), channel_id=1, source_target_pairs={{1,0},{2,1},{3,2},{0,3},{5,4},{6,5},{7,6},{4,7},{9,8},{10,9},{11,1... | collective-permute-start | bytes 3176 | tf_op jit(solution)/shard_map/ppermute | solution.py:15
  29.2 8.6 %collective-permute-start.7 = (f32[4,66,1]{2,1,0:T(8,128)S(1)}, f32[4,66,1]{2,1,0:T(8,128)S(1)}, u32[]{:S(2)}, u32[]{:S(2)}) collective-permute-start(f32[4,66,1]{2,1,0:T(8,128)S(1)} %get-tuple-element.8), channel_id=1, source_target_pairs={{0,1},{1,2},{2,3},{3,0},{4,5},{5,6},{6,7},{7,4},{8,9},{9,10},{10,1... | collective-permute-start | bytes 3176 | tf_op jit(solution)/shard_map/ppermute | solution.py:14
  101.8 37.1 %copy-start.2 = (f32[4,32768]{1,0:T(4,128)S(1)}, f32[4,32768]{1,0:T(4,128)}, u32[]{:S(2)}) copy-start(f32[4,32768]{1,0:T(4,128)} %all-reduce.2.cloned.1.call-done) | copy-start | bytes 1572868
  139.9 34.5 %copy-start.1 = (f32[4,32768]{1,0:T(4,128)S(1)}, f32[4,32768]{1,0:T(4,128)}, u32[]{:S(2)}) copy-start(f32[4,32768]{1,0:T(4,128)} %convolution_select_fusion.1) | copy-start | bytes 1572868
Sparse Core Ops, SparseCore 0:
  76.3 25.4 all-reduce.1
where the time goes:
time: 186 us; the launch traced here: 183 us
  blocking collectives  94.3 us (51%)
  waiting for transfers between devices  43.5 us (23%)
  between operations  14.9 us (8%)
  matrix products  12.4 us (7%)
  starting transfers between devices  9.31 us (5%)
  other arithmetic  6.45 us (3%)
  local copies, waits for them, and re-layouts  2.42 us (1%)
    psum x2, blocking collectives, body(): lax.psum(jnp.dot(flat, flat.T, precision=highest), ('lx', 'ly')) / total  60.7 us
    psum x1, blocking collectives, body(): lax.psum(jnp.dot(shared, flat.T, precision=highest), ('lx', 'ly')) / total  33.6 us
    psum x1, waiting for transfers between devices, from_root(): return lax.psum(kept, axis)  25.6 us
    ppermute x4, waiting for transfers between devices, padded_2(): before = lax.ppermute(last, axis, up)  11.2 us
    ppermute x4, starting transfers between devices, padded_2(): after = lax.ppermute(leading, axis, down)  8.86 us
    ppermute x4, waiting for transfers between devices, padded_2(): after = lax.ppermute(leading, axis, down)  6.71 us
    dot_general x2, matrix products, body(): jnp.dot(flat, flat.T, precision=highest)  4.72 us
  transfers between devices with their start and end apart: 9, of which 7 were waited for; matrix products, arithmetic and copies ran while one was open for 0% of the time, Pallas kernels for 0%

commit v1 on v0

--- a/solution.py
+++ b/solution.py
@@ -1,7 +1,14 @@
+import functools
+
 import jax
 import jax.numpy as jnp
 from jax import lax
+from jax.experimental import pallas as pl
+from jax.experimental.pallas import tpu as pltpu
 from jax.sharding import PartitionSpec as P
+
+MESH_IDS = pl.DeviceIdType.MESH
+SUB, LANE = 8, 128
 
 
 def padded_2(shard, sides, width):
@@ -34,7 +41,7 @@
     return lax.linalg.triangular_solve(lower, eye_block, left_side=True, lower=True)
 
 
-def body(vectors, levels, level_table, filter_low, filter_high):
+def general_body(vectors, levels, level_table, filter_low, filter_high):
     count_vec, rows_local, cols_local = vectors.shape
     level_ids = jnp.arange(level_table.shape[0], dtype=jnp.int32)
     onsite = jnp.sum(
@@ -60,7 +67,330 @@
     return result.reshape(count_vec, rows_local, cols_local)
 
 
+def pair_rows(count):
+    return [(i, j) for i in range(count) for j in range(i + 1)]
+
+
+def lane_ids(shape):
+    return lax.broadcasted_iota(jnp.int32, shape, len(shape) - 1)
+
+
+def inverse_of_factor(gram, size):
+    lower, inverse, recip = {}, {}, []
+    for j in range(size):
+        for i in range(j, size):
+            value = gram[i, j]
+            for k in range(j):
+                value = value - lower[i, k] * lower[j, k]
+            if i == j:
+                recip.append(1.0 / jnp.sqrt(value))
+            else:
+                lower[i, j] = value * recip[j]
+    for j in range(size):
+        inverse[j, j] = recip[j]
+        for i in range(j + 1, size):
+            value = lower[i, j] * inverse[j, j]
+            for k in range(j + 1, i):
+                value = value + lower[i, k] * inverse[k, j]
+            inverse[i, j] = -(value * recip[i])
+    return inverse
+
+
+def kernel(
+    sizes, vec_hbm, lev_hbm, table_ref, low_ref, high_ref, out_hbm,
+    field, level, onsite, filt, other, result,
+    row_send, row_recv, col_send, col_recv, parts, partial, grams, factors,
+    load_sem, halo_send, halo_recv, swap_send, swap_recv, gram_send, gram_recv, store_sem,
+):
+    n_lx, n_ly = sizes
+    count, rows, cols = vec_hbm.shape
+    n_levels = table_ref.shape[0]
+    grp, lx, ly = lax.axis_index("grp"), lax.axis_index("lx"), lax.axis_index("ly")
+    n_all = 2 * n_lx * n_ly
+    me = (grp * n_lx + lx) * n_ly + ly
+    r0, r1, c0, c1 = SUB, SUB + rows, LANE, LANE + cols
+    half_rows = rows // 2
+
+    def place(index):
+        return (index // (n_lx * n_ly), (index // n_ly) % n_lx, index % n_ly)
+
+    loads = [pltpu.make_async_copy(lev_hbm, level, load_sem.at[0])]
+    loads += [
+        pltpu.make_async_copy(vec_hbm.at[v], field.at[v, pl.ds(r0, rows), pl.ds(c0, cols)], load_sem.at[1 + v])
+        for v in range(count)
+    ]
+    for copy in loads:
+        copy.start()
+
+    barrier = pltpu.get_barrier_semaphore()
+    for d in range(1, n_all):
+        pl.semaphore_signal(barrier, inc=1, device_id=place((me + d) % n_all), device_id_type=MESH_IDS)
+
+    for copy in loads:
+        copy.wait()
+
+    lev = level[...]
+    site = jnp.zeros(lev.shape, jnp.float32)
+    for k in range(n_levels):
+        site = jnp.where(lev == k, table_ref[k], site)
+    onsite[r0:r1, c0:c1] = site
+    for v in range(count):
+        row_send[0, 2 * v:2 * v + 2, :] = field[v, r1 - 2:r1, c0:c1]
+        row_send[1, 2 * v:2 * v + 2, :] = field[v, r0:r0 + 2, c0:c1]
+    row_send[0, 2 * count:2 * count + 1, :] = onsite[r1 - 1:r1, c0:c1]
+    row_send[1, 2 * count:2 * count + 1, :] = onsite[r0:r0 + 1, c0:c1]
+    lanes = lane_ids((rows, LANE))
+    ends = onsite[r0:r1, c1 - LANE:c1]
+    begins = onsite[r0:r1, c0:c0 + LANE]
+    right = pltpu.roll(ends, LANE - 2 * count, 1)
+    left = pltpu.roll(begins, 2 * count, 1)
+    for v in range(count):
+        here = field[v, r0:r1, c1 - LANE:c1]
+        here = here if v == 0 else pltpu.roll(here, LANE - 2 * v, 1)
+        right = jnp.where((lanes >= LANE - 2 - 2 * v) & (lanes < LANE - 2 * v), here, right)
+        here = field[v, r0:r1, c0:c0 + LANE]
+        here = here if v == 0 else pltpu.roll(here, 2 * v, 1)
+        left = jnp.where((lanes >= 2 * v) & (lanes < 2 * v + 2), here, left)
+    col_send[0] = right
+    col_send[1] = left
+
+    pl.semaphore_wait(barrier, n_all - 1)
+
+    up, down = (lx + n_lx - 1) % n_lx, (lx + 1) % n_lx
+    west, east = (ly + n_ly - 1) % n_ly, (ly + 1) % n_ly
+    halos = []
+
+    def halo(src, dst, x, y):
+        k = len(halos)
+        copy = pltpu.make_async_remote_copy(
+            src_ref=src, dst_ref=dst, send_sem=halo_send.at[k], recv_sem=halo_recv.at[k],
+            device_id=(grp, x, y), device_id_type=MESH_IDS,
+        )
+        copy.start()
+        halos.append(copy)
+
+    for side, y in ((0, east), (1, west)):
+        halo(col_send.at[side], col_recv.at[side, pl.ds(r0, rows)], lx, y)
+        halo(col_send.at[side, pl.ds(rows - SUB, SUB)], col_recv.at[side, pl.ds(0, SUB)], down, y)
+        halo(col_send.at[side, pl.ds(0, SUB)], col_recv.at[side, pl.ds(r1, SUB)], up, y)
+    halo(row_send.at[0], row_recv.at[0], down, ly)
+    halo(row_send.at[1], row_recv.at[1], up, ly)
+    for copy in halos:
+        copy.wait()
+
+    for v in range(count):
+        field[v, r0 - 2:r0, c0:c1] = row_recv[0, 2 * v:2 * v + 2, :]
+        field[v, r1:r1 + 2, c0:c1] = row_recv[1, 2 * v:2 * v + 2, :]
+        field[v, :, 0:LANE] = pltpu.roll(col_recv[0], 2 * v, 1) if v else col_recv[0]
+        field[v, :, c1:c1 + LANE] = pltpu.roll(col_recv[1], LANE - 2 * v, 1) if v else col_recv[1]
+    onsite[r0 - 1:r0, c0:c1] = row_recv[0, 2 * count:2 * count + 1, :]
+    onsite[r1:r1 + 1, c0:c1] = row_recv[1, 2 * count:2 * count + 1, :]
+    onsite[:, 0:LANE] = pltpu.roll(col_recv[0], 2 * count, 1)
+    onsite[:, c1:c1 + LANE] = pltpu.roll(col_recv[1], LANE - 2 * count, 1)
+
+    low = jnp.full((1, 1), low_ref[0], jnp.float32)
+    high = jnp.full((1, 1), high_ref[0], jnp.float32)
+    center = (high + low) * 0.5
+    scale = 2.0 / (high - low)
+    diagonal = (onsite[...] - center) * scale
+    high_rows, wide = r1 + SUB, c1 + LANE
+
+    def beside(x):
+        return (pltpu.roll(x, 1, 0) + pltpu.roll(x, high_rows - 1, 0)
+                + pltpu.roll(x, 1, 1) + pltpu.roll(x, wide - 1, 1))
+
+    for v in range(count):
+        x = field[v]
+        first = diagonal * x - beside(x) * scale
+        second = 2.0 * (diagonal * first - beside(first) * scale) - x
+        filt[v] = second[r0:r1, c0:c1]
+
+    away = pl.multiple_of((1 - grp) * half_rows, half_rows)
+    near = pl.multiple_of(grp * half_rows, half_rows)
+    swap = pltpu.make_async_remote_copy(
+        src_ref=filt.at[:, pl.ds(away, half_rows)], dst_ref=other.at[:, pl.ds(away, half_rows)],
+        send_sem=swap_send.at[0], recv_sem=swap_recv.at[0],
+        device_id=(1 - grp, lx, ly), device_id_type=MESH_IDS,
+    )
+    swap.start()
+    rest = pltpu.make_async_remote_copy(
+        src_ref=filt.at[:, pl.ds(0, half_rows)], dst_ref=other.at[:, pl.ds(0, half_rows)],
+        send_sem=swap_send.at[1], recv_sem=swap_recv.at[1],
+        device_id=(1 - grp, lx, ly), device_id_type=MESH_IDS,
+    )
+
+    @pl.when(grp == 0)
+    def _():
+        rest.start()
+
+    def folded(a, b):
+        prod = a * b
+        acc = prod[:, 0:LANE]
+        for k in range(1, cols // LANE):
+            acc = acc + prod[:, k * LANE:(k + 1) * LANE]
+        return jnp.sum(acc, axis=0, keepdims=True)
+
+    pairs = pair_rows(count)
+    n_self, n_cross = len(pairs), count * count
+    parts[...] = jnp.zeros(parts.shape, jnp.float32)
+    for p, (i, j) in enumerate(pairs):
+        value = folded(filt[i], filt[j])
+        parts[p:p + 1, :] = jnp.where(grp == 0, value, 0.0)
+        q = n_self + n_cross + p
+        parts[q:q + 1, :] = jnp.where(grp == 0, 0.0, value)
+    swap.wait()
+    cross = {}
+    for a in range(count):
+        for b in range(count):
+            cross[a, b] = folded(filt[a, pl.ds(near, half_rows)], other[b, pl.ds(near, half_rows)])
+    for i in range(count):
+        for j in range(count):
+            p = n_self + i * count + j
+            parts[p:p + 1, :] = jnp.where(grp == 0, cross[j, i], cross[i, j])
+
+    depth = parts.shape[0]
+    diag = lane_ids((depth, LANE)) == lax.broadcasted_iota(jnp.int32, (depth, LANE), 0)
+    sums = jnp.sum(parts[...], axis=1, keepdims=True)
+    packed = jnp.sum(jnp.where(diag, sums, 0.0), axis=0, keepdims=True)
+    partial[0] = packed
+    sends = []
+    for d in range(1, n_all):
+        to = (me + d) % n_all
+        copy = pltpu.make_async_remote_copy(
+            src_ref=partial.at[0], dst_ref=grams.at[me], send_sem=gram_send.at[d], recv_sem=gram_recv.at[me],
+            device_id=place(to), device_id_type=MESH_IDS,
+        )
+        copy.start()
+        sends.append(copy)
+    grams[me] = packed
+    for d in range(1, n_all):
+        source = (me + d) % n_all
+        pltpu.make_async_remote_copy(
+            src_ref=partial.at[0], dst_ref=grams.at[source], send_sem=gram_send.at[d], recv_sem=gram_recv.at[source],
+            device_id=place(source), device_id_type=MESH_IDS,
+        ).wait_recv()
+    total = rows * cols * n_lx * n_ly
+    whole = jnp.sum(grams[...], axis=0) / total
+    column = jnp.sum(jnp.where(diag, whole, 0.0), axis=1, keepdims=True)
+    spread = jnp.broadcast_to(column, (depth, LANE))
+    gram = {}
+    for p, (i, j) in enumerate(pairs):
+        gram[i, j] = spread[p:p + 1]
+        q = n_self + n_cross + p
+        gram[count + i, count + j] = spread[q:q + 1]
+    for i in range(count):
+        for j in range(count):
+            p = n_self + i * count + j
+            gram[count + i, j] = spread[p:p + 1]
+    inverse = inverse_of_factor(gram, 2 * count)
+    for (i, j), value in inverse.items():
+        factors[i, j] = value
+
+    def tiles(start):
+        return [pl.ds(start + k * SUB, SUB) for k in range(half_rows // SUB)]
+
+    def combine(start, with_other):
+        for k in range(half_rows // SUB):
+            at = pl.ds(start + k * SUB, SUB)
+            for t in range(cols // LANE):
+                on = pl.ds(t * LANE, LANE)
+                own = [filt[v, at, on] for v in range(count)]
+                if with_other:
+                    before = [other[v, at, on] for v in range(count)]
+                for i in range(count):
+                    if with_other:
+                        row = count + i
+                        value = factors[row, count] * own[0]
+                        for j in range(1, i + 1):
+                            value = value + factors[row, count + j] * own[j]
+                        for j in range(count):
+                            value = value + factors[row, j] * before[j]
+                    else:
+                        value = factors[i, 0] * own[0]
+                        for j in range(1, i + 1):
+                            value = value + factors[i, j] * own[j]
+                    result[i, at, on] = value
+
+    stores = [
+        pltpu.make_async_copy(
+            result.at[:, pl.ds(s, half_rows)], out_hbm.at[:, pl.ds(s, half_rows)], store_sem.at[k]
+        )
+        for k, s in enumerate((half_rows, 0))
+    ]
+
+    @pl.when(grp == 0)
+    def _():
+        combine(half_rows, False)
+        stores[0].start()
+        combine(0, False)
+        stores[1].start()
+        rest.wait_send()
+
+    @pl.when(grp == 1)
+    def _():
+        combine(half_rows, True)
+        stores[0].start()
+        rest.wait_recv()
+        combine(0, True)
+        stores[1].start()
+
+    for copy in sends:
+        copy.wait_send()
+    for copy in stores:
+        copy.wait()
+
+
+def fused_body(sizes, vectors, levels, level_table, filter_low, filter_high):
+    count, rows, cols = vectors.shape
+    n_all = 2 * sizes[0] * sizes[1]
+    high, wide = rows + 2 * SUB, cols + 2 * LANE
+    n_pairs = count * (2 * count + 1)
+    depth = -(-n_pairs // SUB) * SUB
+    packed_rows = -(-(2 * count + 1) // SUB) * SUB
+    f32 = jnp.float32
+    smem = pl.BlockSpec(memory_space=pltpu.SMEM)
+    anywhere = pl.BlockSpec(memory_space=pl.ANY)
+    dma = pltpu.SemaphoreType.DMA
+    return pl.pallas_call(
+        functools.partial(kernel, sizes),
+        out_shape=jax.ShapeDtypeStruct((count, rows, cols), f32),
+        in_specs=[anywhere, anywhere, smem, smem, smem],
+        out_specs=anywhere,
+        scratch_shapes=[
+            pltpu.VMEM((count, high, wide), f32),
+            pltpu.VMEM((rows, cols), jnp.int32),
+            pltpu.VMEM((high, wide), f32),
+            pltpu.VMEM((count, rows, cols), f32),
+            pltpu.VMEM((count, rows, cols), f32),
+            pltpu.VMEM((count, rows, cols), f32),
+            pltpu.VMEM((2, packed_rows, cols), f32),
+            pltpu.VMEM((2, packed_rows, cols), f32),
+            pltpu.VMEM((2, rows, LANE), f32),
+            pltpu.VMEM((2, high, LANE), f32),
+            pltpu.VMEM((depth, LANE), f32),
+            pltpu.VMEM((1, 1, LANE), f32),
+            pltpu.VMEM((n_all, 1, LANE), f32),
+            pltpu.VMEM((2 * count, 2 * count, 1, LANE), f32),
+            dma((1 + count,)),
+            dma((8,)),
+            dma((8,)),
+            dma((2,)),
+            dma((2,)),
+            dma((n_all,)),
+            dma((n_all,)),
+            dma((2,)),
+        ],
+        compiler_params=pltpu.CompilerParams(
+            collective_id=0, has_side_effects=True, vmem_limit_bytes=32 * 1024 * 1024
+        ),
+    )(vectors, levels, level_table, filter_low, filter_high)
+
+
 def solution(mesh):
     in_specs = (P("grp", "lx", "ly"), P("lx", "ly"), P(), P(), P())
     out_specs = P("grp", "lx", "ly")
+    if mesh.shape["grp"] == 2:
+        body = functools.partial(fused_body, (mesh.shape["lx"], mesh.shape["ly"]))
+    else:
+        body = general_body
     return jax.shard_map(body, mesh=mesh, in_specs=in_specs, out_specs=out_specs, check_vma=False)

time: 186 us -> 31.9 us (0.17)
  the two profiles are of different devices: /device:TPU:2 before, /device:TPU:0 now
where the time goes in v1:
time: 31.9 us; the launch traced here: 31.7 us
  Pallas kernels  27.6 us (87%)
  local copies, waits for them, and re-layouts  2.74 us (9%)
  between operations  1.34 us (4%)
    pallas_call x1, Pallas kernels, fused_body(): pl.pallas_call(functools.partial(kernel, sizes), out_shape=jax.ShapeDtype...  27.6 us
    unnamed x7, local copies, waits for them, and re-layouts  2.74 us

profile of v1, /device:TPU:0, one launch (start us, length us, event | category | flops | bytes accessed | tf_op | source)
XLA Modules:
  0.0 31.7 jit_solution(6809562865856471565)
XLA Ops:
  0.7 0.0 copy-start.2
  1.3 0.0 copy-done.2
  1.3 0.0 copy-start
  1.3 1.0 %copy-done = f32[4,64,512]{2,1,0:T(8,128)S(1)} copy-done((f32[4,64,512]{2,1,0:T(8,128)S(1)}, f32[4,64,512]{2,1,0:T(8,128)}, u32[]{:S(2)}) %copy-start) | copy-done | bytes 524312
  2.4 0.0 copy-start.1
  2.4 0.9 %copy-done.1 = s32[64,512]{1,0:T(8,128)S(1)} copy-done((s32[64,512]{1,0:T(8,128)S(1)}, s32[64,512]{1,0:T(8,128)}, u32[]{:S(2)}) %copy-start.1) | copy-done | bytes 131096
  3.3 27.6 %shard_map.55 = f32[4,64,512]{2,1,0:T(8,128)S(1)} custom-call(f32[4,64,512]{2,1,0:T(8,128)S(1)} %copy-done, s32[64,512]{1,0:T(8,128)S(1)} %copy-done.1, f32[8]{0:T(128)S(1)} %copy-done.2, f32[1]{0:T(128)S(6)} %copy.7.low_ref, f32[1]{0:T(128)S(6)} %copy.8.high_ref), custom_call_target="tpu_custom_call" | custom-call | tf_op jit(solution)/shard_map/pallas_call | solution.py:354
  30.9 0.8 %copy.9 = f32[4,64,512]{2,1,0:T(8,128)} copy(f32[4,64,512]{2,1,0:T(8,128)S(1)} %shard_map.55) | data formatting | bytes 1048576
Async XLA Ops:
  0.7 0.7 %copy-start.2 = (f32[8]{0:T(128)S(1)}, f32[8]{0:T(128)}, u32[]{:S(2)}) copy-start(f32[8]{0:T(128)} %table_ref.1) | copy-start | bytes 100
  1.3 1.0 %copy-start = (f32[4,64,512]{2,1,0:T(8,128)S(1)}, f32[4,64,512]{2,1,0:T(8,128)}, u32[]{:S(2)}) copy-start(f32[4,64,512]{2,1,0:T(8,128)} %vec_hbm.1) | copy-start | bytes 1572868
  2.4 0.9 %copy-start.1 = (s32[64,512]{1,0:T(8,128)S(1)}, s32[64,512]{1,0:T(8,128)}, u32[]{:S(2)}) copy-start(s32[64,512]{1,0:T(8,128)} %lev_hbm.1) | copy-start | bytes 393220

commit v2 on v1

--- a/solution.py
+++ b/solution.py
@@ -97,8 +97,8 @@
 
 
 def kernel(
-    sizes, vec_hbm, lev_hbm, table_ref, low_ref, high_ref, out_hbm,
-    field, level, onsite, filt, other, result,
+    sizes, vec_hbm, lev_hbm, table_hbm, low_hbm, high_hbm, out_hbm,
+    table_ref, low_ref, high_ref, field, level, onsite, filt, other, result,
     row_send, row_recv, col_send, col_recv, parts, partial, grams, factors,
     load_sem, halo_send, halo_recv, swap_send, swap_recv, gram_send, gram_recv, store_sem,
 ):
@@ -115,6 +115,10 @@
         return (index // (n_lx * n_ly), (index // n_ly) % n_lx, index % n_ly)
 
     loads = [pltpu.make_async_copy(lev_hbm, level, load_sem.at[0])]
+    loads += [
+        pltpu.make_async_copy(src, dst, load_sem.at[1 + count + k])
+        for k, (src, dst) in enumerate(((table_hbm, table_ref), (low_hbm, low_ref), (high_hbm, high_ref)))
+    ]
     loads += [
         pltpu.make_async_copy(vec_hbm.at[v], field.at[v, pl.ds(r0, rows), pl.ds(c0, cols)], load_sem.at[1 + v])
         for v in range(count)
@@ -348,15 +352,17 @@
     depth = -(-n_pairs // SUB) * SUB
     packed_rows = -(-(2 * count + 1) // SUB) * SUB
     f32 = jnp.float32
-    smem = pl.BlockSpec(memory_space=pltpu.SMEM)
     anywhere = pl.BlockSpec(memory_space=pl.ANY)
     dma = pltpu.SemaphoreType.DMA
     return pl.pallas_call(
         functools.partial(kernel, sizes),
         out_shape=jax.ShapeDtypeStruct((count, rows, cols), f32),
-        in_specs=[anywhere, anywhere, smem, smem, smem],
+        in_specs=[anywhere] * 5,
         out_specs=anywhere,
         scratch_shapes=[
+            pltpu.SMEM(level_table.shape, f32),
+            pltpu.SMEM(filter_low.shape, f32),
+            pltpu.SMEM(filter_high.shape, f32),
             pltpu.VMEM((count, high, wide), f32),
             pltpu.VMEM((rows, cols), jnp.int32),
             pltpu.VMEM((high, wide), f32),
@@ -371,7 +377,7 @@
             pltpu.VMEM((1, 1, LANE), f32),
             pltpu.VMEM((n_all, 1, LANE), f32),
             pltpu.VMEM((2 * count, 2 * count, 1, LANE), f32),
-            dma((1 + count,)),
+            dma((4 + count,)),
             dma((8,)),
             dma((8,)),
             dma((2,)),
@@ -381,7 +387,7 @@
             dma((2,)),
         ],
         compiler_params=pltpu.CompilerParams(
-            collective_id=0, has_side_effects=True, vmem_limit_bytes=32 * 1024 * 1024
+            collective_id=0, has_side_effects=True, vmem_limit_bytes=60 * 1024 * 1024
         ),
     )(vectors, levels, level_table, filter_low, filter_high)
 

time: 31.9 us -> 30.9 us (0.969)
  local copies, waits for them, and re-layouts: 2.74 us -> 1.87 us
    unnamed x7 -> x1, local copies, waits for them, and re-layouts: 2.74 us -> 1.87 us
where the time goes in v2:
time: 30.9 us; the launch traced here: 30.7 us
  Pallas kernels  27.5 us (89%)
  local copies, waits for them, and re-layouts  1.87 us (6%)
  between operations  1.3 us (4%)
    pallas_call x1, Pallas kernels, fused_body(): pl.pallas_call(functools.partial(kernel, sizes), out_shape=jax.ShapeDtype...  27.5 us
    unnamed x1, local copies, waits for them, and re-layouts  1.87 us

profile of v2, /device:TPU:0, one launch (start us, length us, event | category | flops | bytes accessed | tf_op | source)
XLA Modules:
  0.0 30.7 jit_solution(12254685876074837323)
XLA Ops:
  1.3 27.5 %shard_map.55 = f32[4,64,512]{2,1,0:T(8,128)} custom-call(f32[4,64,512]{2,1,0:T(8,128)} %vec_hbm.1, s32[64,512]{1,0:T(8,128)} %lev_hbm.1, f32[8]{0:T(128)} %table_hbm.1, f32[1]{0:T(128)S(6)} %copy.7.low_hbm, f32[1]{0:T(128)S(6)} %copy.8.high_hbm), custom_call_target="tpu_custom_call" | custom-call | tf_op jit(solution)/shard_map/pallas_call | solution.py:357
  28.8 1.9 %copy.9 = f32[4,64,512]{2,1,0:T(8,128)} copy(f32[4,64,512]{2,1,0:T(8,128)} %shard_map.55) | data formatting | bytes 1048576

commit v3 on v0

--- a/solution.py
+++ b/solution.py
@@ -1,7 +1,14 @@
+import functools
+
 import jax
 import jax.numpy as jnp
 from jax import lax
+from jax.experimental import pallas as pl
+from jax.experimental.pallas import tpu as pltpu
 from jax.sharding import PartitionSpec as P
+
+MESH_IDS = pl.DeviceIdType.MESH
+SUB, LANE = 8, 128
 
 
 def padded_2(shard, sides, width):
@@ -34,7 +41,7 @@
     return lax.linalg.triangular_solve(lower, eye_block, left_side=True, lower=True)
 
 
-def body(vectors, levels, level_table, filter_low, filter_high):
+def general_body(vectors, levels, level_table, filter_low, filter_high):
     count_vec, rows_local, cols_local = vectors.shape
     level_ids = jnp.arange(level_table.shape[0], dtype=jnp.int32)
     onsite = jnp.sum(
@@ -60,7 +67,392 @@
     return result.reshape(count_vec, rows_local, cols_local)
 
 
+def pair_rows(count):
+    return [(i, j) for i in range(count) for j in range(i + 1)]
+
+
+def lane_ids(shape):
+    return lax.broadcasted_iota(jnp.int32, shape, len(shape) - 1)
+
+
+def inverse_of_factor(gram, size):
+    lower, inverse, recip = {}, {}, []
+    for j in range(size):
+        for i in range(j, size):
+            value = gram[i, j]
+            for k in range(j):
+                value = value - lower[i, k] * lower[j, k]
+            if i == j:
+                recip.append(1.0 / jnp.sqrt(value))
+            else:
+                lower[i, j] = value * recip[j]
+    for j in range(size):
+        inverse[j, j] = recip[j]
+        for i in range(j + 1, size):
+            value = lower[i, j] * inverse[j, j]
+            for k in range(j + 1, i):
+                value = value + lower[i, k] * inverse[k, j]
+            inverse[i, j] = -(value * recip[i])
+    return inverse
+
+
+def kernel(
+    sizes, vec_hbm, lev_hbm, table_hbm, low_ref, high_ref, out_hbm,
+    table_ref, field, level, onsite, filt, mate, other, result,
+    row_send, row_recv, col_send, col_recv, fold, mate_rows, mate_fold, mate_cols,
+    parts, partial, early, grams, factors,
+    load_sem, halo_send, halo_recv, grp_send, grp_recv, early_send, early_recv, gram_send, gram_recv, store_sem,
+):
+    n_lx, n_ly = sizes
+    count, rows, cols = vec_hbm.shape
+    n_levels = table_hbm.shape[0]
+    grp, lx, ly = lax.axis_index("grp"), lax.axis_index("lx"), lax.axis_index("ly")
+    n_plane = n_lx * n_ly
+    spot = lx * n_ly + ly
+    me = grp * n_plane + spot
+    r0, r1, c0, c1 = SUB, SUB + rows, LANE, LANE + cols
+    high, wide = r1 + SUB, c1 + LANE
+    split = rows * 3 // 8 // SUB * SUB
+
+    def place(block, index):
+        index = index % n_plane
+        return (block, index // n_ly, index % n_ly)
+
+    def remote(src, dst, send, recv, to):
+        return pltpu.make_async_remote_copy(
+            src_ref=src, dst_ref=dst, send_sem=send, recv_sem=recv, device_id=to, device_id_type=MESH_IDS
+        )
+
+    loads = [pltpu.make_async_copy(lev_hbm, level, load_sem.at[0])]
+    loads += [pltpu.make_async_copy(table_hbm, table_ref, load_sem.at[1])]
+    loads += [
+        pltpu.make_async_copy(vec_hbm.at[v], field.at[v, pl.ds(r0, rows), pl.ds(c0, cols)], load_sem.at[2 + v])
+        for v in range(count)
+    ]
+    for copy in loads:
+        copy.start()
+
+    barrier = pltpu.get_barrier_semaphore()
+    for d in range(1, n_plane):
+        pl.semaphore_signal(barrier, inc=1, device_id=place(grp, spot + d), device_id_type=MESH_IDS)
+    pl.semaphore_signal(barrier, inc=1, device_id=(1 - grp, lx, ly), device_id_type=MESH_IDS)
+
+    @pl.when(grp == 1)
+    def _():
+        for d in range(1, n_plane):
+            pl.semaphore_signal(barrier, inc=1, device_id=place(0, spot + d), device_id_type=MESH_IDS)
+
+    for copy in loads:
+        copy.wait()
+
+    lev = level[...]
+    site = jnp.zeros(lev.shape, jnp.float32)
+    for k in range(n_levels):
+        site = jnp.where(lev == k, table_ref[k], site)
+    onsite[r0:r1, c0:c1] = site
+    for v in range(count):
+        row_send[0, 2 * v:2 * v + 2, :] = field[v, r1 - 2:r1, c0:c1]
+        row_send[1, 2 * v:2 * v + 2, :] = field[v, r0:r0 + 2, c0:c1]
+    row_send[0, 2 * count:2 * count + 1, :] = onsite[r1 - 1:r1, c0:c1]
+    row_send[1, 2 * count:2 * count + 1, :] = onsite[r0:r0 + 1, c0:c1]
+    lanes = lane_ids((rows, LANE))
+    ends = onsite[r0:r1, c1 - LANE:c1]
+    begins = onsite[r0:r1, c0:c0 + LANE]
+    right = pltpu.roll(ends, LANE - 2 * count, 1)
+    left = pltpu.roll(begins, 2 * count, 1)
+    for v in range(count):
+        here = field[v, r0:r1, c1 - LANE:c1]
+        here = here if v == 0 else pltpu.roll(here, LANE - 2 * v, 1)
+        right = jnp.where((lanes >= LANE - 2 - 2 * v) & (lanes < LANE - 2 * v), here, right)
+        here = field[v, r0:r1, c0:c0 + LANE]
+        here = here if v == 0 else pltpu.roll(here, 2 * v, 1)
+        left = jnp.where((lanes >= 2 * v) & (lanes < 2 * v + 2), here, left)
+    col_send[0] = right
+    col_send[1] = left
+
+    @pl.when(grp == 0)
+    def _():
+        pl.semaphore_wait(barrier, 2 * n_plane - 1)
+
+    @pl.when(grp == 1)
+    def _():
+        pl.semaphore_wait(barrier, n_plane)
+
+    up, down = (lx + n_lx - 1) % n_lx, (lx + 1) % n_lx
+    west, east = (ly + n_ly - 1) % n_ly, (ly + 1) % n_ly
+    halos = []
+
+    def halo(src, dst, x, y):
+        k = len(halos)
+        copy = remote(src, dst, halo_send.at[k], halo_recv.at[k], (grp, x, y))
+        copy.start()
+        halos.append(copy)
+
+    for side, y in ((0, east), (1, west)):
+        halo(col_send.at[side], col_recv.at[side, pl.ds(r0, rows)], lx, y)
+        halo(col_send.at[side, pl.ds(rows - SUB, SUB)], col_recv.at[side, pl.ds(0, SUB)], down, y)
+        halo(col_send.at[side, pl.ds(0, SUB)], col_recv.at[side, pl.ds(r1, SUB)], up, y)
+    halo(row_send.at[0], row_recv.at[0], down, ly)
+    halo(row_send.at[1], row_recv.at[1], up, ly)
+
+    partner = (1 - grp, lx, ly)
+    n_link = [0]
+
+    def across(src, dst):
+        k = n_link[0]
+        n_link[0] += 1
+        return remote(src, dst, grp_send.at[k], grp_recv.at[k], partner)
+
+    def band(start, stop):
+        at = (slice(None), pl.ds(r0 + start, stop - start), pl.ds(c0, cols))
+        return across(field.at[at], mate.at[at])
+
+    lower = band(split - SUB, rows)
+    upper = band(0, split - SUB)
+    edges = [across(row_recv.at[k, pl.ds(0, 2 * count)], mate_rows.at[k]) for k in range(2)]
+    edges.append(across(fold, mate_fold))
+    back = across(filt.at[:, pl.ds(0, split)], other.at[:, pl.ds(0, split)])
+
+    @pl.when(grp == 0)
+    def _():
+        lower.start()
+
+    for copy in halos:
+        copy.wait()
+
+    group = 4 * count
+    per_tile = LANE // group
+    tile_lanes = lane_ids((SUB, LANE))
+
+    @pl.when(grp == 0)
+    def _():
+        for t in range(fold.shape[0] // SUB):
+            value = jnp.zeros((SUB, LANE), jnp.float32)
+            for g in range(per_tile):
+                at = (t * per_tile + g) * SUB
+                if at >= high:
+                    break
+                both = jnp.where(tile_lanes < LANE // 2, col_recv[1, at:at + SUB], col_recv[0, at:at + SUB])
+                both = pltpu.roll(both, 2 * count + group * g, 1)
+                value = jnp.where((tile_lanes >= group * g) & (tile_lanes < group * (g + 1)), both, value)
+            fold[t * SUB:(t + 1) * SUB] = value
+        for copy in edges:
+            copy.start()
+        upper.start()
+
+    def place_edges(dst, first_rows, last_rows, before, after):
+        for v in range(count):
+            dst[v, r0 - 2:r0, c0:c1] = first_rows[2 * v:2 * v + 2, :]
+            dst[v, r1:r1 + 2, c0:c1] = last_rows[2 * v:2 * v + 2, :]
+            dst[v, :, 0:LANE] = pltpu.roll(before[...], 2 * v, 1) if v else before[...]
+            dst[v, :, c1:c1 + LANE] = pltpu.roll(after[...], LANE - 2 * v, 1) if v else after[...]
+
+    place_edges(field, row_recv.at[0], row_recv.at[1], col_recv.at[0], col_recv.at[1])
+    low = jnp.full((1, 1), low_ref[0], jnp.float32)
+    top = jnp.full((1, 1), high_ref[0], jnp.float32)
+    center = (top + low) * 0.5
+    scale = 2.0 / (top - low)
+    onsite[r0 - 1:r0, c0:c1] = row_recv[0, 2 * count:2 * count + 1, :]
+    onsite[r1:r1 + 1, c0:c1] = row_recv[1, 2 * count:2 * count + 1, :]
+    onsite[:, 0:LANE] = pltpu.roll(col_recv[0], 2 * count, 1)
+    onsite[:, c1:c1 + LANE] = pltpu.roll(col_recv[1], LANE - 2 * count, 1)
+    onsite[...] = (onsite[...] - center) * scale
+
+    def filter_rows(src, dst, start, stop):
+        at = pl.ds(start, stop - start + 2 * SUB)
+        n = stop - start + 2 * SUB
+        diagonal = onsite[at, :]
+
+        def beside(x):
+            return (pltpu.roll(x, 1, 0) + pltpu.roll(x, n - 1, 0)
+                    + pltpu.roll(x, 1, 1) + pltpu.roll(x, wide - 1, 1))
+
+        for v in range(count):
+            x = src[v, at, :]
+            first = diagonal * x - beside(x) * scale
+            second = 2.0 * (diagonal * first - beside(first) * scale) - x
+            dst[v, start:stop] = second[SUB:SUB + stop - start, c0:c1]
+
+    filter_rows(field, filt, 0, rows)
+
+    @pl.when(grp == 1)
+    def _():
+        back.start()
+
+    pairs = pair_rows(count)
+    n_self, n_cross = len(pairs), count * count
+    depth = parts.shape[0]
+    diag = lane_ids((depth, LANE)) == lax.broadcasted_iota(jnp.int32, (depth, LANE), 0)
+    total = rows * cols * n_lx * n_ly
+
+    def folded(a, b):
+        prod = a * b
+        acc = prod[:, 0:LANE]
+        for k in range(1, cols // LANE):
+            acc = acc + prod[:, k * LANE:(k + 1) * LANE]
+        return jnp.sum(acc, axis=0, keepdims=True)
+
+    def packed_parts():
+        sums = jnp.sum(parts[...], axis=1, keepdims=True)
+        return jnp.sum(jnp.where(diag, sums, 0.0), axis=0, keepdims=True)
+
+    def spread_out(slots):
+        whole = jnp.sum(slots[...], axis=0) / total
+        column = jnp.sum(jnp.where(diag, whole, 0.0), axis=1, keepdims=True)
+        return jnp.broadcast_to(column, (depth, LANE))
+
+    def keep_factor(gram, size):
+        for (i, j), value in inverse_of_factor(gram, size).items():
+            factors[i, j] = value
+
+    parts[...] = jnp.zeros(parts.shape, jnp.float32)
+    for p, (i, j) in enumerate(pairs):
+        value = folded(filt[i], filt[j])
+        parts[p:p + 1, :] = jnp.where(grp == 0, value, 0.0)
+        q = n_self + n_cross + p
+        parts[q:q + 1, :] = jnp.where(grp == 0, 0.0, value)
+
+    def cross_parts(block_0, block_1, start, stop):
+        for i in range(count):
+            for j in range(count):
+                p = n_self + i * count + j
+                parts[p:p + 1, :] = folded(block_1[i, start:stop], block_0[j, start:stop])
+
+    def combine(start, stop, first_row, blocks):
+        for at_row in range(start, stop, SUB):
+            at = pl.ds(at_row, SUB)
+            for t in range(cols // LANE):
+                on = pl.ds(t * LANE, LANE)
+                tiles = [block[v, at, on] for block in blocks for v in range(count)]
+                for i in range(count):
+                    row = first_row + i
+                    value = factors[row, 0] * tiles[0]
+                    for j in range(1, row + 1):
+                        value = value + factors[row, j] * tiles[j]
+                    result[i, at, on] = value
+
+    middle = rows // 2 // SUB * SUB
+    halves = ((0, middle), (middle, rows))
+    stores = [
+        pltpu.make_async_copy(result.at[:, pl.ds(s, e - s)], out_hbm.at[:, pl.ds(s, e - s)], store_sem.at[k])
+        for k, (s, e) in enumerate(halves)
+    ]
+
+    def finish(first_row, blocks):
+        for store, (s, e) in zip(stores, halves):
+            combine(s, e, first_row, blocks)
+            store.start()
+
+    @pl.when(grp == 0)
+    def _():
+        partial[0] = packed_parts()
+        early[spot] = partial[0]
+        sends = []
+        for d in range(1, n_plane):
+            copy = remote(partial.at[0], early.at[spot], early_send.at[d], early_recv.at[spot], place(0, spot + d))
+            copy.start()
+            sends.append(copy)
+        for d in range(1, n_plane):
+            source = (spot + d) % n_plane
+            remote(partial.at[0], early.at[source], early_send.at[d], early_recv.at[source], place(0, source)).wait_recv()
+        spread = spread_out(early)
+        keep_factor({(i, j): spread[p:p + 1] for p, (i, j) in enumerate(pairs)}, count)
+        finish(0, [filt])
+        back.wait_recv()
+        cross_parts(filt, other, 0, split)
+        partial[1] = packed_parts()
+        for d in range(n_plane):
+            copy = remote(partial.at[1], grams.at[me], gram_send.at[d], gram_recv.at[me], place(1, spot + d))
+            copy.start()
+            sends.append(copy)
+        for copy in [lower, upper] + edges + sends:
+            copy.wait_send()
+
+    @pl.when(grp == 1)
+    def _():
+        for copy in edges:
+            copy.wait_recv()
+        for k in range(high // SUB):
+            t, g = k // per_tile, k % per_tile
+            tile = mate_fold[t * SUB:(t + 1) * SUB]
+            mate_cols[k * SUB:(k + 1) * SUB] = pltpu.roll(tile, LANE - 2 * count - group * g, 1)
+        place_edges(mate, mate_rows.at[0], mate_rows.at[1], mate_cols, mate_cols)
+        lower.wait_recv()
+        filter_rows(mate, other, split, rows)
+        cross_parts(other, filt, split, rows)
+        partial[1] = packed_parts()
+        grams[me] = partial[1]
+        sends = []
+        for d in range(1, n_plane):
+            copy = remote(partial.at[1], grams.at[me], gram_send.at[d], gram_recv.at[me], place(1, spot + d))
+            copy.start()
+            sends.append(copy)
+        upper.wait_recv()
+        filter_rows(mate, other, 0, split)
+        for d in range(1, 2 * n_plane):
+            source = (me + d) % (2 * n_plane)
+            remote(
+                partial.at[1], grams.at[source], gram_send.at[0], gram_recv.at[source],
+                place(source // n_plane, source),
+            ).wait_recv()
+        spread = spread_out(grams)
+        gram = {}
+        for p, (i, j) in enumerate(pairs):
+            gram[i, j] = spread[p:p + 1]
+            q = n_self + n_cross + p
+            gram[count + i, count + j] = spread[q:q + 1]
+        for i in range(count):
+            for j in range(count):
+                p = n_self + i * count + j
+                gram[count + i, j] = spread[p:p + 1]
+        keep_factor(gram, 2 * count)
+        finish(count, [other, filt])
+        for copy in [back] + sends:
+            copy.wait_send()
+
+    for copy in stores:
+        copy.wait()
+
+
+def fused_body(sizes, vectors, levels, level_table, filter_low, filter_high):
+    count, rows, cols = vectors.shape
+    n_plane = sizes[0] * sizes[1]
+    high, wide = rows + 2 * SUB, cols + 2 * LANE
+    depth = -(-count * (2 * count + 1) // SUB) * SUB
+    packed_rows = -(-(2 * count + 1) // SUB) * SUB
+    fold_rows = -(-(high // SUB) // (LANE // (4 * count))) * SUB
+    f32 = jnp.float32
+    anywhere = pl.BlockSpec(memory_space=pl.ANY)
+    in_smem = pl.BlockSpec(memory_space=pltpu.SMEM)
+    dma = pltpu.SemaphoreType.DMA
+    block = (count, rows, cols)
+    padded = (count, high, wide)
+    vmem_shapes = [
+        padded, None, (high, wide), block, padded, block, block,
+        (2, packed_rows, cols), (2, packed_rows, cols), (2, rows, LANE), (2, high, LANE),
+        (fold_rows, LANE), (2, 2 * count, cols), (fold_rows, LANE), (high, LANE),
+        (depth, LANE), (2, 1, LANE), (n_plane, 1, LANE), (2 * n_plane, 1, LANE),
+        (2 * count, 2 * count, 1, LANE),
+    ]
+    scratch = [pltpu.VMEM(s, f32) if s else pltpu.VMEM((rows, cols), jnp.int32) for s in vmem_shapes]
+    counts = (2 + count, 8, 8, 6, 6, n_plane, n_plane, n_plane, 2 * n_plane, 2)
+    return pl.pallas_call(
+        functools.partial(kernel, sizes),
+        out_shape=jax.ShapeDtypeStruct(block, f32),
+        in_specs=[anywhere] * 3 + [in_smem] * 2,
+        out_specs=anywhere,
+        scratch_shapes=[pltpu.SMEM(level_table.shape, f32)] + scratch + [dma((n,)) for n in counts],
+        compiler_params=pltpu.CompilerParams(
+            collective_id=0, has_side_effects=True, vmem_limit_bytes=60 * 1024 * 1024
+        ),
+    )(vectors, levels, level_table, filter_low, filter_high)
+
+
 def solution(mesh):
     in_specs = (P("grp", "lx", "ly"), P("lx", "ly"), P(), P(), P())
     out_specs = P("grp", "lx", "ly")
+    if mesh.shape["grp"] == 2:
+        body = functools.partial(fused_body, (mesh.shape["lx"], mesh.shape["ly"]))
+    else:
+        body = general_body
     return jax.shard_map(body, mesh=mesh, in_specs=in_specs, out_specs=out_specs, check_vma=False)

time: 186 us -> 27 us (0.15); the launches traced: 183 us -> 26.8 us
  blocking collectives: 94.3 us -> 0 us
  waiting for transfers between devices: 43.5 us -> 0 us
  Pallas kernels: 0 us -> 23.6 us
  between operations: 14.9 us -> 1.3 us
  matrix products: 12.4 us -> 0 us
  starting transfers between devices: 9.31 us -> 0 us
  other arithmetic: 6.45 us -> 0 us
    psum x3 -> x0, blocking collectives: 94.3 us -> none  [the longest x2 60.7 us: body(): lax.psum(jnp.dot(flat, flat.T, precision=highest), ('lx', 'ly')) / total]
    psum x1 -> x0, waiting for transfers between devices: 25.6 us -> none  [from_root(): return lax.psum(kept, axis)]
    pallas_call x0 -> x1, Pallas kernels: none -> 23.6 us  [fused_body(): pl.pallas_call(functools.partial(kernel, sizes), out_shape=jax.ShapeDtype...]
    ppermute x8 -> x0, waiting for transfers between devices: 17.9 us -> none  [the longest x4 11.2 us: padded_2(): before = lax.ppermute(last, axis, up)]
    dot_general x6 -> x0, matrix products: 12 us -> none  [the longest x2 4.72 us: body(): jnp.dot(flat, flat.T, precision=highest)]
    ppermute x8 -> x0, starting transfers between devices: 9.3 us -> none  [the longest x4 8.86 us: padded_2(): after = lax.ppermute(leading, axis, down)]
    another operation x10 -> x0, other arithmetic: 4.17 us -> none  [the longest x6 2.15 us: lower_inverse(): lower = jnp.linalg.cholesky(gram)]
  transfers between devices with their start and end apart: 9 -> 0, of which waited for: 7 -> 0; matrix products, arithmetic and copies ran while one was open for 0% -> 0% of each run, Pallas kernels for 0% -> 0%
where the time goes in v3:
time: 27 us; the launch traced here: 26.8 us
  Pallas kernels  23.6 us (87%)
  local copies, waits for them, and re-layouts  1.87 us (7%)
  between operations  1.3 us (5%)
    pallas_call x1, Pallas kernels, fused_body(): pl.pallas_call(functools.partial(kernel, sizes), out_shape=jax.ShapeDtype...  23.6 us
    unnamed x1, local copies, waits for them, and re-layouts  1.87 us

profile of v3, /device:TPU:2, one launch (start us, length us, event | category | flops | bytes accessed | tf_op | source)
XLA Modules:
  0.0 26.8 jit_solution(4356615959755893713)
XLA Ops:
  1.3 23.6 %shard_map.55 = f32[4,64,512]{2,1,0:T(8,128)} custom-call(f32[4,64,512]{2,1,0:T(8,128)} %vec_hbm.1, s32[64,512]{1,0:T(8,128)} %lev_hbm.1, f32[8]{0:T(128)} %table_hbm.1, f32[1]{0:T(128)S(6)} %copy.7.low_ref, f32[1]{0:T(128)S(6)} %copy.8.high_ref), custom_call_target="tpu_custom_call" | custom-call | tf_op jit(solution)/shard_map/pallas_call | solution.py:439
  24.9 1.9 %copy.9 = f32[4,64,512]{2,1,0:T(8,128)} copy(f32[4,64,512]{2,1,0:T(8,128)} %shard_map.55) | data formatting | bytes 1048576

commit v4 on v3

--- a/solution.py
+++ b/solution.py
@@ -75,6 +75,11 @@
     return lax.broadcasted_iota(jnp.int32, shape, len(shape) - 1)
 
 
+def turned(tile, shift):
+    shift = shift % LANE
+    return pltpu.roll(tile, shift, 1) if shift else tile
+
+
 def inverse_of_factor(gram, size):
     lower, inverse, recip = {}, {}, []
     for j in range(size):
@@ -97,11 +102,11 @@
 
 
 def kernel(
-    sizes, vec_hbm, lev_hbm, table_hbm, low_ref, high_ref, out_hbm,
-    table_ref, field, level, onsite, filt, mate, other, result,
-    row_send, row_recv, col_send, col_recv, fold, mate_rows, mate_fold, mate_cols,
+    sizes, vec_hbm, lev_hbm, table_hbm, low_ref, high_ref, result,
+    table_ref, field, level, onsite, filt, mate, other,
+    row_send, row_recv, col_send, col_recv, edge_cols, mate_rows, mate_fold, mate_cols,
     parts, partial, early, grams, factors,
-    load_sem, halo_send, halo_recv, grp_send, grp_recv, early_send, early_recv, gram_send, gram_recv, store_sem,
+    load_sem, halo_send, halo_recv, grp_send, grp_recv, early_send, early_recv, gram_send, gram_recv,
 ):
     n_lx, n_ly = sizes
     count, rows, cols = vec_hbm.shape
@@ -112,7 +117,10 @@
     me = grp * n_plane + spot
     r0, r1, c0, c1 = SUB, SUB + rows, LANE, LANE + cols
     high, wide = r1 + SUB, c1 + LANE
-    split = rows * 3 // 8 // SUB * SUB
+    split = rows // 2 // SUB * SUB
+    group = 2 * SUB
+    per_tile = LANE // group
+    bands = rows // SUB
 
     def place(block, index):
         index = index % n_plane
@@ -167,8 +175,15 @@
         here = field[v, r0:r1, c0:c0 + LANE]
         here = here if v == 0 else pltpu.roll(here, 2 * v, 1)
         left = jnp.where((lanes >= 2 * v) & (lanes < 2 * v + 2), here, left)
-    col_send[0] = right
-    col_send[1] = left
+    tile_lanes = lane_ids((SUB, LANE))
+    for side, edge in enumerate((right, left)):
+        for t in range(col_send.shape[1] // SUB):
+            value = jnp.zeros((SUB, LANE), jnp.float32)
+            for k in range(t * per_tile, min(bands, (t + 1) * per_tile)):
+                at = group * (k - t * per_tile)
+                tile = turned(edge[k * SUB:(k + 1) * SUB], at + group * (1 - side))
+                value = jnp.where((tile_lanes >= at) & (tile_lanes < at + group), tile, value)
+            col_send[side, t * SUB:(t + 1) * SUB] = value
 
     @pl.when(grp == 0)
     def _():
@@ -189,9 +204,8 @@
         halos.append(copy)
 
     for side, y in ((0, east), (1, west)):
-        halo(col_send.at[side], col_recv.at[side, pl.ds(r0, rows)], lx, y)
-        halo(col_send.at[side, pl.ds(rows - SUB, SUB)], col_recv.at[side, pl.ds(0, SUB)], down, y)
-        halo(col_send.at[side, pl.ds(0, SUB)], col_recv.at[side, pl.ds(r1, SUB)], up, y)
+        for slot, x in enumerate((lx, down, up)):
+            halo(col_send.at[side], col_recv.at[side, slot], x, y)
     halo(row_send.at[0], row_recv.at[0], down, ly)
     halo(row_send.at[1], row_recv.at[1], up, ly)
 
@@ -209,36 +223,34 @@
 
     lower = band(split - SUB, rows)
     upper = band(0, split - SUB)
-    edges = [across(row_recv.at[k, pl.ds(0, 2 * count)], mate_rows.at[k]) for k in range(2)]
-    edges.append(across(fold, mate_fold))
-    back = across(filt.at[:, pl.ds(0, split)], other.at[:, pl.ds(0, split)])
+    back = band(0, split + SUB)
+    edges = [across(row_recv.at[:, pl.ds(0, 2 * count)], mate_rows), across(col_recv, mate_fold)]
 
     @pl.when(grp == 0)
     def _():
         lower.start()
+
+    @pl.when(grp == 1)
+    def _():
+        back.start()
 
     for copy in halos:
         copy.wait()
 
-    group = 4 * count
-    per_tile = LANE // group
-    tile_lanes = lane_ids((SUB, LANE))
+    for copy in edges:
+        copy.start()
 
     @pl.when(grp == 0)
     def _():
-        for t in range(fold.shape[0] // SUB):
-            value = jnp.zeros((SUB, LANE), jnp.float32)
-            for g in range(per_tile):
-                at = (t * per_tile + g) * SUB
-                if at >= high:
-                    break
-                both = jnp.where(tile_lanes < LANE // 2, col_recv[1, at:at + SUB], col_recv[0, at:at + SUB])
-                both = pltpu.roll(both, 2 * count + group * g, 1)
-                value = jnp.where((tile_lanes >= group * g) & (tile_lanes < group * (g + 1)), both, value)
-            fold[t * SUB:(t + 1) * SUB] = value
-        for copy in edges:
-            copy.start()
         upper.start()
+
+    def unfold(src, dst):
+        for side in range(2):
+            for k in range(bands + 2):
+                slot, band_at = (1, bands - 1) if k == 0 else (2, 0) if k == bands + 1 else (0, k - 1)
+                t, g = band_at // per_tile, band_at % per_tile
+                tile = src[side, slot, t * SUB:(t + 1) * SUB]
+                dst[side, k * SUB:(k + 1) * SUB] = turned(tile, -group * (g + 1 - side))
 
     def place_edges(dst, first_rows, last_rows, before, after):
         for v in range(count):
@@ -247,15 +259,16 @@
             dst[v, :, 0:LANE] = pltpu.roll(before[...], 2 * v, 1) if v else before[...]
             dst[v, :, c1:c1 + LANE] = pltpu.roll(after[...], LANE - 2 * v, 1) if v else after[...]
 
-    place_edges(field, row_recv.at[0], row_recv.at[1], col_recv.at[0], col_recv.at[1])
+    unfold(col_recv, edge_cols)
+    place_edges(field, row_recv.at[0], row_recv.at[1], edge_cols.at[0], edge_cols.at[1])
     low = jnp.full((1, 1), low_ref[0], jnp.float32)
     top = jnp.full((1, 1), high_ref[0], jnp.float32)
     center = (top + low) * 0.5
     scale = 2.0 / (top - low)
     onsite[r0 - 1:r0, c0:c1] = row_recv[0, 2 * count:2 * count + 1, :]
     onsite[r1:r1 + 1, c0:c1] = row_recv[1, 2 * count:2 * count + 1, :]
-    onsite[:, 0:LANE] = pltpu.roll(col_recv[0], 2 * count, 1)
-    onsite[:, c1:c1 + LANE] = pltpu.roll(col_recv[1], LANE - 2 * count, 1)
+    onsite[:, 0:LANE] = pltpu.roll(edge_cols[0], 2 * count, 1)
+    onsite[:, c1:c1 + LANE] = pltpu.roll(edge_cols[1], LANE - 2 * count, 1)
     onsite[...] = (onsite[...] - center) * scale
 
     def filter_rows(src, dst, start, stop):
@@ -274,10 +287,6 @@
             dst[v, start:stop] = second[SUB:SUB + stop - start, c0:c1]
 
     filter_rows(field, filt, 0, rows)
-
-    @pl.when(grp == 1)
-    def _():
-        back.start()
 
     pairs = pair_rows(count)
     n_self, n_cross = len(pairs), count * count
@@ -331,17 +340,11 @@
                         value = value + factors[row, j] * tiles[j]
                     result[i, at, on] = value
 
-    middle = rows // 2 // SUB * SUB
-    halves = ((0, middle), (middle, rows))
-    stores = [
-        pltpu.make_async_copy(result.at[:, pl.ds(s, e - s)], out_hbm.at[:, pl.ds(s, e - s)], store_sem.at[k])
-        for k, (s, e) in enumerate(halves)
-    ]
-
-    def finish(first_row, blocks):
-        for store, (s, e) in zip(stores, halves):
-            combine(s, e, first_row, blocks)
-            store.start()
+    def place_mate_edges():
+        for copy in edges:
+            copy.wait_recv()
+        unfold(mate_fold, mate_cols)
+        place_edges(mate, mate_rows.at[0], mate_rows.at[1], mate_cols.at[0], mate_cols.at[1])
 
     @pl.when(grp == 0)
     def _():
@@ -352,31 +355,27 @@
             copy = remote(partial.at[0], early.at[spot], early_send.at[d], early_recv.at[spot], place(0, spot + d))
             copy.start()
             sends.append(copy)
-        for d in range(1, n_plane):
-            source = (spot + d) % n_plane
-            remote(partial.at[0], early.at[source], early_send.at[d], early_recv.at[source], place(0, source)).wait_recv()
-        spread = spread_out(early)
-        keep_factor({(i, j): spread[p:p + 1] for p, (i, j) in enumerate(pairs)}, count)
-        finish(0, [filt])
+        place_mate_edges()
         back.wait_recv()
+        filter_rows(mate, other, 0, split)
         cross_parts(filt, other, 0, split)
         partial[1] = packed_parts()
         for d in range(n_plane):
             copy = remote(partial.at[1], grams.at[me], gram_send.at[d], gram_recv.at[me], place(1, spot + d))
             copy.start()
             sends.append(copy)
+        for d in range(1, n_plane):
+            source = (spot + d) % n_plane
+            remote(partial.at[0], early.at[source], early_send.at[d], early_recv.at[source], place(0, source)).wait_recv()
+        spread = spread_out(early)
+        keep_factor({(i, j): spread[p:p + 1] for p, (i, j) in enumerate(pairs)}, count)
+        combine(0, rows, 0, [filt])
         for copy in [lower, upper] + edges + sends:
             copy.wait_send()
 
     @pl.when(grp == 1)
     def _():
-        for copy in edges:
-            copy.wait_recv()
-        for k in range(high // SUB):
-            t, g = k // per_tile, k % per_tile
-            tile = mate_fold[t * SUB:(t + 1) * SUB]
-            mate_cols[k * SUB:(k + 1) * SUB] = pltpu.roll(tile, LANE - 2 * count - group * g, 1)
-        place_edges(mate, mate_rows.at[0], mate_rows.at[1], mate_cols, mate_cols)
+        place_mate_edges()
         lower.wait_recv()
         filter_rows(mate, other, split, rows)
         cross_parts(other, filt, split, rows)
@@ -406,12 +405,9 @@
                 p = n_self + i * count + j
                 gram[count + i, j] = spread[p:p + 1]
         keep_factor(gram, 2 * count)
-        finish(count, [other, filt])
-        for copy in [back] + sends:
+        combine(0, rows, count, [other, filt])
+        for copy in [back] + edges + sends:
             copy.wait_send()
-
-    for copy in stores:
-        copy.wait()
 
 
 def fused_body(sizes, vectors, levels, level_table, filter_low, filter_high):
@@ -420,7 +416,7 @@
     high, wide = rows + 2 * SUB, cols + 2 * LANE
     depth = -(-count * (2 * count + 1) // SUB) * SUB
     packed_rows = -(-(2 * count + 1) // SUB) * SUB
-    fold_rows = -(-(high // SUB) // (LANE // (4 * count))) * SUB
+    fold_rows = -(-(rows // SUB) // (LANE // (2 * SUB))) * SUB
     f32 = jnp.float32
     anywhere = pl.BlockSpec(memory_space=pl.ANY)
     in_smem = pl.BlockSpec(memory_space=pltpu.SMEM)
@@ -428,19 +424,19 @@
     block = (count, rows, cols)
     padded = (count, high, wide)
     vmem_shapes = [
-        padded, None, (high, wide), block, padded, block, block,
-        (2, packed_rows, cols), (2, packed_rows, cols), (2, rows, LANE), (2, high, LANE),
-        (fold_rows, LANE), (2, 2 * count, cols), (fold_rows, LANE), (high, LANE),
+        padded, None, (high, wide), block, padded, block,
+        (2, packed_rows, cols), (2, packed_rows, cols), (2, fold_rows, LANE), (2, 3, fold_rows, LANE),
+        (2, high, LANE), (2, 2 * count, cols), (2, 3, fold_rows, LANE), (2, high, LANE),
         (depth, LANE), (2, 1, LANE), (n_plane, 1, LANE), (2 * n_plane, 1, LANE),
         (2 * count, 2 * count, 1, LANE),
     ]
     scratch = [pltpu.VMEM(s, f32) if s else pltpu.VMEM((rows, cols), jnp.int32) for s in vmem_shapes]
-    counts = (2 + count, 8, 8, 6, 6, n_plane, n_plane, n_plane, 2 * n_plane, 2)
+    counts = (2 + count, 8, 8, 5, 5, n_plane, n_plane, n_plane, 2 * n_plane)
     return pl.pallas_call(
         functools.partial(kernel, sizes),
-        out_shape=jax.ShapeDtypeStruct(block, f32),
+        out_shape=pltpu.VMEM(block, f32),
         in_specs=[anywhere] * 3 + [in_smem] * 2,
-        out_specs=anywhere,
+        out_specs=pl.BlockSpec(memory_space=pltpu.VMEM),
         scratch_shapes=[pltpu.SMEM(level_table.shape, f32)] + scratch + [dma((n,)) for n in counts],
         compiler_params=pltpu.CompilerParams(
             collective_id=0, has_side_effects=True, vmem_limit_bytes=60 * 1024 * 1024

time: 27 us -> 24.6 us (0.911)
  Pallas kernels: 23.6 us -> 22.4 us
  local copies, waits for them, and re-layouts: 1.87 us -> 0.8 us
    pallas_call x1, Pallas kernels: 23.6 us -> 22.4 us  [fused_body(): pl.pallas_call(functools.partial(kernel, sizes), out_shape=pltpu.VMEM(blo...]
    unnamed x1, local copies, waits for them, and re-layouts: 1.87 us -> 0.8 us
where the time goes in v4:
time: 24.6 us; the launch traced here: 24.5 us
  Pallas kernels  22.4 us (91%)
  between operations  1.3 us (5%)
  local copies, waits for them, and re-layouts  0.8 us (3%)
    pallas_call x1, Pallas kernels, fused_body(): pl.pallas_call(functools.partial(kernel, sizes), out_shape=pltpu.VMEM(blo...  22.4 us
    unnamed x1, local copies, waits for them, and re-layouts  0.8 us

profile of v4, /device:TPU:2, one launch (start us, length us, event | category | flops | bytes accessed | tf_op | source)
XLA Modules:
  0.0 24.5 jit_solution(4177839367315337459)
XLA Ops:
  1.3 22.4 %shard_map.55 = f32[4,64,512]{2,1,0:T(8,128)S(1)} custom-call(f32[4,64,512]{2,1,0:T(8,128)} %vec_hbm.1, s32[64,512]{1,0:T(8,128)} %lev_hbm.1, f32[8]{0:T(128)} %table_hbm.1, f32[1]{0:T(128)S(6)} %copy.8.low_ref, f32[1]{0:T(128)S(6)} %copy.9.high_ref), custom_call_target="tpu_custom_call" | custom-call | tf_op jit(solution)/shard_map/pallas_call | solution.py:435
  23.7 0.8 %copy.7 = f32[4,64,512]{2,1,0:T(8,128)} copy(f32[4,64,512]{2,1,0:T(8,128)S(1)} %shard_map.55) | data formatting | bytes 1048576

commit v5 on v4

--- a/solution.py
+++ b/solution.py
@@ -118,6 +118,7 @@
     r0, r1, c0, c1 = SUB, SUB + rows, LANE, LANE + cols
     high, wide = r1 + SUB, c1 + LANE
     split = rows // 2 // SUB * SUB
+    last = split // 2 // SUB * SUB
     group = 2 * SUB
     per_tile = LANE // group
     bands = rows // SUB
@@ -137,7 +138,7 @@
         pltpu.make_async_copy(vec_hbm.at[v], field.at[v, pl.ds(r0, rows), pl.ds(c0, cols)], load_sem.at[2 + v])
         for v in range(count)
     ]
-    for copy in loads:
+    for copy in loads[2:] + loads[:2]:
         copy.start()
 
     barrier = pltpu.get_barrier_semaphore()
@@ -150,7 +151,44 @@
         for d in range(1, n_plane):
             pl.semaphore_signal(barrier, inc=1, device_id=place(0, spot + d), device_id_type=MESH_IDS)
 
-    for copy in loads:
+    for copy in loads[2:]:
+        copy.wait()
+
+    @pl.when(grp == 0)
+    def _():
+        pl.semaphore_wait(barrier, 2 * n_plane - 1)
+
+    @pl.when(grp == 1)
+    def _():
+        pl.semaphore_wait(barrier, n_plane)
+
+    partner = (1 - grp, lx, ly)
+    n_link = [0]
+
+    def across(src, dst):
+        k = n_link[0]
+        n_link[0] += 1
+        return remote(src, dst, grp_send.at[k], grp_recv.at[k], partner)
+
+    def band(start, stop):
+        at = (slice(None), pl.ds(r0 + start, stop - start), pl.ds(c0, cols))
+        return across(field.at[at], mate.at[at])
+
+    lower = band(split - SUB, rows)
+    middle = band(last - SUB, split - SUB)
+    upper = band(0, last - SUB)
+    back = band(0, split + SUB)
+    edges = [across(row_recv.at[:, pl.ds(0, 2 * count)], mate_rows), across(col_recv, mate_fold)]
+
+    @pl.when(grp == 0)
+    def _():
+        lower.start()
+
+    @pl.when(grp == 1)
+    def _():
+        back.start()
+
+    for copy in loads[:2]:
         copy.wait()
 
     lev = level[...]
@@ -185,14 +223,6 @@
                 value = jnp.where((tile_lanes >= at) & (tile_lanes < at + group), tile, value)
             col_send[side, t * SUB:(t + 1) * SUB] = value
 
-    @pl.when(grp == 0)
-    def _():
-        pl.semaphore_wait(barrier, 2 * n_plane - 1)
-
-    @pl.when(grp == 1)
-    def _():
-        pl.semaphore_wait(barrier, n_plane)
-
     up, down = (lx + n_lx - 1) % n_lx, (lx + 1) % n_lx
     west, east = (ly + n_ly - 1) % n_ly, (ly + 1) % n_ly
     halos = []
@@ -209,31 +239,6 @@
     halo(row_send.at[0], row_recv.at[0], down, ly)
     halo(row_send.at[1], row_recv.at[1], up, ly)
 
-    partner = (1 - grp, lx, ly)
-    n_link = [0]
-
-    def across(src, dst):
-        k = n_link[0]
-        n_link[0] += 1
-        return remote(src, dst, grp_send.at[k], grp_recv.at[k], partner)
-
-    def band(start, stop):
-        at = (slice(None), pl.ds(r0 + start, stop - start), pl.ds(c0, cols))
-        return across(field.at[at], mate.at[at])
-
-    lower = band(split - SUB, rows)
-    upper = band(0, split - SUB)
-    back = band(0, split + SUB)
-    edges = [across(row_recv.at[:, pl.ds(0, 2 * count)], mate_rows), across(col_recv, mate_fold)]
-
-    @pl.when(grp == 0)
-    def _():
-        lower.start()
-
-    @pl.when(grp == 1)
-    def _():
-        back.start()
-
     for copy in halos:
         copy.wait()
 
@@ -242,6 +247,7 @@
 
     @pl.when(grp == 0)
     def _():
+        middle.start()
         upper.start()
 
     def unfold(src, dst):
@@ -370,7 +376,7 @@
         spread = spread_out(early)
         keep_factor({(i, j): spread[p:p + 1] for p, (i, j) in enumerate(pairs)}, count)
         combine(0, rows, 0, [filt])
-        for copy in [lower, upper] + edges + sends:
+        for copy in [lower, middle, upper] + edges + sends:
             copy.wait_send()
 
     @pl.when(grp == 1)
@@ -386,8 +392,8 @@
             copy = remote(partial.at[1], grams.at[me], gram_send.at[d], gram_recv.at[me], place(1, spot + d))
             copy.start()
             sends.append(copy)
-        upper.wait_recv()
-        filter_rows(mate, other, 0, split)
+        middle.wait_recv()
+        filter_rows(mate, other, last, split)
         for d in range(1, 2 * n_plane):
             source = (me + d) % (2 * n_plane)
             remote(
@@ -405,7 +411,10 @@
                 p = n_self + i * count + j
                 gram[count + i, j] = spread[p:p + 1]
         keep_factor(gram, 2 * count)
-        combine(0, rows, count, [other, filt])
+        combine(last, rows, count, [other, filt])
+        upper.wait_recv()
+        filter_rows(mate, other, 0, last)
+        combine(0, last, count, [other, filt])
         for copy in [back] + edges + sends:
             copy.wait_send()
 
@@ -431,7 +440,7 @@
         (2 * count, 2 * count, 1, LANE),
     ]
     scratch = [pltpu.VMEM(s, f32) if s else pltpu.VMEM((rows, cols), jnp.int32) for s in vmem_shapes]
-    counts = (2 + count, 8, 8, 5, 5, n_plane, n_plane, n_plane, 2 * n_plane)
+    counts = (2 + count, 8, 8, 6, 6, n_plane, n_plane, n_plane, 2 * n_plane)
     return pl.pallas_call(
         functools.partial(kernel, sizes),
         out_shape=pltpu.VMEM(block, f32),

time: 24.6 us -> 24.6 us (level); the launches traced: 24.5 us -> 24.2 us
  Pallas kernels: 22.4 us -> 22.1 us
    pallas_call x1, Pallas kernels: 22.4 us -> 22.1 us  [fused_body(): pl.pallas_call(functools.partial(kernel, sizes), out_shape=pltpu.VMEM(blo...]
where the time goes in v5:
time: 24.6 us; the launch traced here: 24.2 us
  Pallas kernels  22.1 us (90%)
  between operations  1.3 us (5%)
  local copies, waits for them, and re-layouts  0.8 us (3%)
    pallas_call x1, Pallas kernels, fused_body(): pl.pallas_call(functools.partial(kernel, sizes), out_shape=pltpu.VMEM(blo...  22.1 us
    unnamed x1, local copies, waits for them, and re-layouts  0.8 us

profile of v5, /device:TPU:2, one launch (start us, length us, event | category | flops | bytes accessed | tf_op | source)
XLA Modules:
  0.0 24.2 jit_solution(9797813672944390233)
XLA Ops:
  1.3 22.1 %shard_map.55 = f32[4,64,512]{2,1,0:T(8,128)S(1)} custom-call(f32[4,64,512]{2,1,0:T(8,128)} %vec_hbm.1, s32[64,512]{1,0:T(8,128)} %lev_hbm.1, f32[8]{0:T(128)} %table_hbm.1, f32[1]{0:T(128)S(6)} %copy.8.low_ref, f32[1]{0:T(128)S(6)} %copy.9.high_ref), custom_call_target="tpu_custom_call" | custom-call | tf_op jit(solution)/shard_map/pallas_call | solution.py:444
  23.4 0.8 %copy.7 = f32[4,64,512]{2,1,0:T(8,128)} copy(f32[4,64,512]{2,1,0:T(8,128)S(1)} %shard_map.55) | data formatting | bytes 1048576

commit v6 on v5

--- a/solution.py
+++ b/solution.py
@@ -103,8 +103,8 @@
 
 def kernel(
     sizes, vec_hbm, lev_hbm, table_hbm, low_ref, high_ref, result,
-    table_ref, field, level, onsite, filt, mate, other,
-    row_send, row_recv, col_send, col_recv, edge_cols, mate_rows, mate_fold, mate_cols,
+    table_ref, field, level, onsite, filt, near, far, other,
+    row_send, row_recv, col_send, col_recv, edge_cols, mate_rows, mate_fold, mate_cols, seam_send, seam_recv,
     parts, partial, early, grams, factors,
     load_sem, halo_send, halo_recv, grp_send, grp_recv, early_send, early_recv, gram_send, gram_recv,
 ):
@@ -117,7 +117,7 @@
     me = grp * n_plane + spot
     r0, r1, c0, c1 = SUB, SUB + rows, LANE, LANE + cols
     high, wide = r1 + SUB, c1 + LANE
-    split = rows // 2 // SUB * SUB
+    split = rows // 2
     last = split // 2 // SUB * SUB
     group = 2 * SUB
     per_tile = LANE // group
@@ -171,22 +171,29 @@
         return remote(src, dst, grp_send.at[k], grp_recv.at[k], partner)
 
     def band(start, stop):
-        at = (slice(None), pl.ds(r0 + start, stop - start), pl.ds(c0, cols))
-        return across(field.at[at], mate.at[at])
-
-    lower = band(split - SUB, rows)
-    middle = band(last - SUB, split - SUB)
+        from_rows, to_rows = pl.ds(r0 + start, stop - start), pl.ds(SUB + start, stop - start)
+        return across(field.at[:, from_rows, pl.ds(c0, cols)], far.at[:, to_rows, pl.ds(c0, cols)])
+
+    sent = pl.multiple_of(r0 + (1 - grp) * split, SUB)
+    nearest = across(
+        field.at[:, pl.ds(sent, split), pl.ds(c0, cols)], near.at[:, pl.ds(SUB, split), pl.ds(c0, cols)]
+    )
+    middle = band(last - SUB, split)
     upper = band(0, last - SUB)
-    back = band(0, split + SUB)
-    edges = [across(row_recv.at[:, pl.ds(0, 2 * count)], mate_rows), across(col_recv, mate_fold)]
-
-    @pl.when(grp == 0)
-    def _():
-        lower.start()
-
-    @pl.when(grp == 1)
-    def _():
-        back.start()
+    packed_two = pl.ds(0, 2 * count)
+    seam = across(seam_send, seam_recv)
+    edges = [
+        across(col_recv, mate_fold),
+        across(row_recv.at[1 - grp, packed_two], mate_rows.at[1 - grp]),
+    ]
+    far_edge = across(row_recv.at[0, packed_two], mate_rows.at[0])
+
+    nearest.start()
+    for v in range(count):
+        seam_send[2 * v:2 * v + 2, :] = jnp.where(
+            grp == 0, field[v, r0 + split - 2:r0 + split, c0:c1], field[v, r0 + split:r0 + split + 2, c0:c1]
+        )
+    seam.start()
 
     for copy in loads[:2]:
         copy.wait()
@@ -247,6 +254,7 @@
 
     @pl.when(grp == 0)
     def _():
+        far_edge.start()
         middle.start()
         upper.start()
 
@@ -258,15 +266,21 @@
                 tile = src[side, slot, t * SUB:(t + 1) * SUB]
                 dst[side, k * SUB:(k + 1) * SUB] = turned(tile, -group * (g + 1 - side))
 
-    def place_edges(dst, first_rows, last_rows, before, after):
+    def place_rows(dst, at, src):
         for v in range(count):
-            dst[v, r0 - 2:r0, c0:c1] = first_rows[2 * v:2 * v + 2, :]
-            dst[v, r1:r1 + 2, c0:c1] = last_rows[2 * v:2 * v + 2, :]
-            dst[v, :, 0:LANE] = pltpu.roll(before[...], 2 * v, 1) if v else before[...]
-            dst[v, :, c1:c1 + LANE] = pltpu.roll(after[...], LANE - 2 * v, 1) if v else after[...]
+            dst[v, at:at + 2, c0:c1] = src[2 * v:2 * v + 2, :]
+
+    def place_cols(dst, src, start):
+        n = dst.shape[1]
+        before, after = src[0, start:start + n], src[1, start:start + n]
+        for v in range(count):
+            dst[v, :, 0:LANE] = turned(before, 2 * v)
+            dst[v, :, c1:c1 + LANE] = turned(after, -2 * v)
 
     unfold(col_recv, edge_cols)
-    place_edges(field, row_recv.at[0], row_recv.at[1], edge_cols.at[0], edge_cols.at[1])
+    place_rows(field, r0 - 2, row_recv.at[0])
+    place_rows(field, r1, row_recv.at[1])
+    place_cols(field, edge_cols, 0)
     low = jnp.full((1, 1), low_ref[0], jnp.float32)
     top = jnp.full((1, 1), high_ref[0], jnp.float32)
     center = (top + low) * 0.5
@@ -277,8 +291,9 @@
     onsite[:, c1:c1 + LANE] = pltpu.roll(edge_cols[1], LANE - 2 * count, 1)
     onsite[...] = (onsite[...] - center) * scale
 
-    def filter_rows(src, dst, start, stop):
+    def filter_rows(src, dst, start, stop, base=0):
         at = pl.ds(start, stop - start + 2 * SUB)
+        at_src = pl.ds(start - base, stop - start + 2 * SUB)
         n = stop - start + 2 * SUB
         diagonal = onsite[at, :]
 
@@ -287,7 +302,7 @@
                     + pltpu.roll(x, 1, 1) + pltpu.roll(x, wide - 1, 1))
 
         for v in range(count):
-            x = src[v, at, :]
+            x = src[v, at_src, :]
             first = diagonal * x - beside(x) * scale
             second = 2.0 * (diagonal * first - beside(first) * scale) - x
             dst[v, start:stop] = second[SUB:SUB + stop - start, c0:c1]
@@ -315,6 +330,9 @@
         whole = jnp.sum(slots[...], axis=0) / total
         column = jnp.sum(jnp.where(diag, whole, 0.0), axis=1, keepdims=True)
         return jnp.broadcast_to(column, (depth, LANE))
+
+    def whole_tile(spread, p):
+        return jnp.broadcast_to(spread[p:p + 1], (SUB, LANE))
 
     def keep_factor(gram, size):
         for (i, j), value in inverse_of_factor(gram, size).items():
@@ -346,11 +364,15 @@
                         value = value + factors[row, j] * tiles[j]
                     result[i, at, on] = value
 
-    def place_mate_edges():
+    def place_near(start, first_rows, last_rows):
+        nearest.wait_recv()
+        seam.wait_recv()
         for copy in edges:
             copy.wait_recv()
         unfold(mate_fold, mate_cols)
-        place_edges(mate, mate_rows.at[0], mate_rows.at[1], mate_cols.at[0], mate_cols.at[1])
+        place_cols(near, mate_cols, start)
+        place_rows(near, SUB - 2, first_rows)
+        place_rows(near, SUB + split, last_rows)
 
     @pl.when(grp == 0)
     def _():
@@ -361,9 +383,8 @@
             copy = remote(partial.at[0], early.at[spot], early_send.at[d], early_recv.at[spot], place(0, spot + d))
             copy.start()
             sends.append(copy)
-        place_mate_edges()
-        back.wait_recv()
-        filter_rows(mate, other, 0, split)
+        place_near(0, mate_rows.at[0], seam_recv)
+        filter_rows(near, other, 0, split)
         cross_parts(filt, other, 0, split)
         partial[1] = packed_parts()
         for d in range(n_plane):
@@ -374,16 +395,15 @@
             source = (spot + d) % n_plane
             remote(partial.at[0], early.at[source], early_send.at[d], early_recv.at[source], place(0, source)).wait_recv()
         spread = spread_out(early)
-        keep_factor({(i, j): spread[p:p + 1] for p, (i, j) in enumerate(pairs)}, count)
+        keep_factor({(i, j): whole_tile(spread, p) for p, (i, j) in enumerate(pairs)}, count)
         combine(0, rows, 0, [filt])
-        for copy in [lower, middle, upper] + edges + sends:
+        for copy in [nearest, seam, far_edge, middle, upper] + edges + sends:
             copy.wait_send()
 
     @pl.when(grp == 1)
     def _():
-        place_mate_edges()
-        lower.wait_recv()
-        filter_rows(mate, other, split, rows)
+        place_near(split, seam_recv, mate_rows.at[1])
+        filter_rows(near, other, split, rows, split)
         cross_parts(other, filt, split, rows)
         partial[1] = packed_parts()
         grams[me] = partial[1]
@@ -392,8 +412,13 @@
             copy = remote(partial.at[1], grams.at[me], gram_send.at[d], gram_recv.at[me], place(1, spot + d))
             copy.start()
             sends.append(copy)
+        far_edge.wait_recv()
+        place_cols(far, mate_cols, 0)
+        place_rows(far, SUB - 2, mate_rows.at[0])
+        for v in range(count):
+            far[v, SUB + split:SUB + split + 2, c0:c1] = near[v, SUB:SUB + 2, c0:c1]
         middle.wait_recv()
-        filter_rows(mate, other, last, split)
+        filter_rows(far, other, last, split)
         for d in range(1, 2 * n_plane):
             source = (me + d) % (2 * n_plane)
             remote(
@@ -403,19 +428,19 @@
         spread = spread_out(grams)
         gram = {}
         for p, (i, j) in enumerate(pairs):
-            gram[i, j] = spread[p:p + 1]
+            gram[i, j] = whole_tile(spread, p)
             q = n_self + n_cross + p
-            gram[count + i, count + j] = spread[q:q + 1]
+            gram[count + i, count + j] = whole_tile(spread, q)
         for i in range(count):
             for j in range(count):
                 p = n_self + i * count + j
-                gram[count + i, j] = spread[p:p + 1]
+                gram[count + i, j] = whole_tile(spread, p)
         keep_factor(gram, 2 * count)
         combine(last, rows, count, [other, filt])
         upper.wait_recv()
-        filter_rows(mate, other, 0, last)
+        filter_rows(far, other, 0, last)
         combine(0, last, count, [other, filt])
-        for copy in [back] + edges + sends:
+        for copy in [nearest, seam] + edges + sends:
             copy.wait_send()
 
 
@@ -431,16 +456,17 @@
     in_smem = pl.BlockSpec(memory_space=pltpu.SMEM)
     dma = pltpu.SemaphoreType.DMA
     block = (count, rows, cols)
-    padded = (count, high, wide)
+    padded, part = (count, high, wide), (count, rows // 2 + 2 * SUB, wide)
     vmem_shapes = [
-        padded, None, (high, wide), block, padded, block,
+        padded, None, (high, wide), block, part, part, block,
         (2, packed_rows, cols), (2, packed_rows, cols), (2, fold_rows, LANE), (2, 3, fold_rows, LANE),
         (2, high, LANE), (2, 2 * count, cols), (2, 3, fold_rows, LANE), (2, high, LANE),
+        (2 * count, cols), (2 * count, cols),
         (depth, LANE), (2, 1, LANE), (n_plane, 1, LANE), (2 * n_plane, 1, LANE),
-        (2 * count, 2 * count, 1, LANE),
+        (2 * count, 2 * count, SUB, LANE),
     ]
     scratch = [pltpu.VMEM(s, f32) if s else pltpu.VMEM((rows, cols), jnp.int32) for s in vmem_shapes]
-    counts = (2 + count, 8, 8, 6, 6, n_plane, n_plane, n_plane, 2 * n_plane)
+    counts = (2 + count, 8, 8, 7, 7, n_plane, n_plane, n_plane, 2 * n_plane)
     return pl.pallas_call(
         functools.partial(kernel, sizes),
         out_shape=pltpu.VMEM(block, f32),
@@ -456,8 +482,13 @@
 def solution(mesh):
     in_specs = (P("grp", "lx", "ly"), P("lx", "ly"), P(), P(), P())
     out_specs = P("grp", "lx", "ly")
-    if mesh.shape["grp"] == 2:
-        body = functools.partial(fused_body, (mesh.shape["lx"], mesh.shape["ly"]))
-    else:
-        body = general_body
+    sizes = (mesh.shape["lx"], mesh.shape["ly"])
+
+    def body(vectors, *others):
+        count, rows, cols = vectors.shape
+        fits = count == 4 and rows % (4 * SUB) == 0 and cols % LANE == 0
+        if mesh.shape["grp"] == 2 and fits and rows >= 8 * SUB:
+            return fused_body(sizes, vectors, *others)
+        return general_body(vectors, *others)
+
     return jax.shard_map(body, mesh=mesh, in_specs=in_specs, out_specs=out_specs, check_vma=False)

time: 24.6 us -> 24.9 us (1.012)
  Pallas kernels: 22.1 us -> 22.4 us
    pallas_call x1, Pallas kernels: 22.1 us -> 22.4 us  [fused_body(): pl.pallas_call(functools.partial(kernel, sizes), out_shape=pltpu.VMEM(blo...]
where the time goes in v6:
time: 24.9 us; the launch traced here: 24.5 us
  Pallas kernels  22.4 us (90%)
  between operations  1.3 us (5%)
  local copies, waits for them, and re-layouts  0.8 us (3%)
    pallas_call x1, Pallas kernels, fused_body(): pl.pallas_call(functools.partial(kernel, sizes), out_shape=pltpu.VMEM(blo...  22.4 us
    unnamed x1, local copies, waits for them, and re-layouts  0.8 us

profile of v6, /device:TPU:2, one launch (start us, length us, event | category | flops | bytes accessed | tf_op | source)
XLA Modules:
  0.0 24.5 jit_solution(2281539457704788276)
XLA Ops:
  1.3 22.4 %shard_map.55 = f32[4,64,512]{2,1,0:T(8,128)S(1)} custom-call(f32[4,64,512]{2,1,0:T(8,128)} %vec_hbm.1, s32[64,512]{1,0:T(8,128)} %lev_hbm.1, f32[8]{0:T(128)} %table_hbm.1, f32[1]{0:T(128)S(6)} %copy.8.low_ref, f32[1]{0:T(128)S(6)} %copy.9.high_ref), custom_call_target="tpu_custom_call" | custom-call | tf_op jit(solution)/shard_map/pallas_call | solution.py:470
  23.7 0.8 %copy.7 = f32[4,64,512]{2,1,0:T(8,128)} copy(f32[4,64,512]{2,1,0:T(8,128)S(1)} %shard_map.55) | data formatting | bytes 1048576

commit v7 on v6

--- a/solution.py
+++ b/solution.py
@@ -116,7 +116,7 @@
     spot = lx * n_ly + ly
     me = grp * n_plane + spot
     r0, r1, c0, c1 = SUB, SUB + rows, LANE, LANE + cols
-    high, wide = r1 + SUB, c1 + LANE
+    high, wide = r1 + SUB, c1
     split = rows // 2
     last = split // 2 // SUB * SUB
     group = 2 * SUB
@@ -270,12 +270,14 @@
         for v in range(count):
             dst[v, at:at + 2, c0:c1] = src[2 * v:2 * v + 2, :]
 
+    def joined(before, after):
+        return jnp.where(lane_ids(before.shape) < LANE // 2, after, before)
+
     def place_cols(dst, src, start):
         n = dst.shape[1]
         before, after = src[0, start:start + n], src[1, start:start + n]
         for v in range(count):
-            dst[v, :, 0:LANE] = turned(before, 2 * v)
-            dst[v, :, c1:c1 + LANE] = turned(after, -2 * v)
+            dst[v, :, 0:LANE] = joined(turned(before, 2 * v), turned(after, -2 * v))
 
     unfold(col_recv, edge_cols)
     place_rows(field, r0 - 2, row_recv.at[0])
@@ -287,8 +289,7 @@
     scale = 2.0 / (top - low)
     onsite[r0 - 1:r0, c0:c1] = row_recv[0, 2 * count:2 * count + 1, :]
     onsite[r1:r1 + 1, c0:c1] = row_recv[1, 2 * count:2 * count + 1, :]
-    onsite[:, 0:LANE] = pltpu.roll(edge_cols[0], 2 * count, 1)
-    onsite[:, c1:c1 + LANE] = pltpu.roll(edge_cols[1], LANE - 2 * count, 1)
+    onsite[:, 0:LANE] = joined(turned(edge_cols[0], 2 * count), turned(edge_cols[1], -2 * count))
     onsite[...] = (onsite[...] - center) * scale
 
     def filter_rows(src, dst, start, stop, base=0):
@@ -365,7 +366,6 @@
                     result[i, at, on] = value
 
     def place_near(start, first_rows, last_rows):
-        nearest.wait_recv()
         seam.wait_recv()
         for copy in edges:
             copy.wait_recv()
@@ -373,6 +373,7 @@
         place_cols(near, mate_cols, start)
         place_rows(near, SUB - 2, first_rows)
         place_rows(near, SUB + split, last_rows)
+        nearest.wait_recv()
 
     @pl.when(grp == 0)
     def _():
@@ -419,6 +420,8 @@
             far[v, SUB + split:SUB + split + 2, c0:c1] = near[v, SUB:SUB + 2, c0:c1]
         middle.wait_recv()
         filter_rows(far, other, last, split)
+        for copy in [nearest, seam] + edges + sends:
+            copy.wait_send()
         for d in range(1, 2 * n_plane):
             source = (me + d) % (2 * n_plane)
             remote(
@@ -440,14 +443,12 @@
         upper.wait_recv()
         filter_rows(far, other, 0, last)
         combine(0, last, count, [other, filt])
-        for copy in [nearest, seam] + edges + sends:
-            copy.wait_send()
 
 
 def fused_body(sizes, vectors, levels, level_table, filter_low, filter_high):
     count, rows, cols = vectors.shape
     n_plane = sizes[0] * sizes[1]
-    high, wide = rows + 2 * SUB, cols + 2 * LANE
+    high, wide = rows + 2 * SUB, cols + LANE
     depth = -(-count * (2 * count + 1) // SUB) * SUB
     packed_rows = -(-(2 * count + 1) // SUB) * SUB
     fold_rows = -(-(rows // SUB) // (LANE // (2 * SUB))) * SUB

time: 24.9 us -> 24.9 us (level)
  no operation moved by 1% of the time
where the time goes in v7:
time: 24.9 us; the launch traced here: 24.5 us
  Pallas kernels  22.4 us (90%)
  between operations  1.3 us (5%)
  local copies, waits for them, and re-layouts  0.8 us (3%)
    pallas_call x1, Pallas kernels, fused_body(): pl.pallas_call(functools.partial(kernel, sizes), out_shape=pltpu.VMEM(blo...  22.4 us
    unnamed x1, local copies, waits for them, and re-layouts  0.8 us

profile of v7, /device:TPU:2, one launch (start us, length us, event | category | flops | bytes accessed | tf_op | source)
XLA Modules:
  0.0 24.5 jit_solution(15859652174535510931)
XLA Ops:
  1.3 22.4 %shard_map.55 = f32[4,64,512]{2,1,0:T(8,128)S(1)} custom-call(f32[4,64,512]{2,1,0:T(8,128)} %vec_hbm.1, s32[64,512]{1,0:T(8,128)} %lev_hbm.1, f32[8]{0:T(128)} %table_hbm.1, f32[1]{0:T(128)S(6)} %copy.8.low_ref, f32[1]{0:T(128)S(6)} %copy.9.high_ref), custom_call_target="tpu_custom_call" | custom-call | tf_op jit(solution)/shard_map/pallas_call | solution.py:471
  23.7 0.8 %copy.7 = f32[4,64,512]{2,1,0:T(8,128)} copy(f32[4,64,512]{2,1,0:T(8,128)S(1)} %shard_map.55) | data formatting | bytes 1048576

commit v8 on v7

--- a/solution.py
+++ b/solution.py
@@ -256,7 +256,6 @@
     def _():
         far_edge.start()
         middle.start()
-        upper.start()
 
     def unfold(src, dst):
         for side in range(2):
@@ -392,6 +391,7 @@
             copy = remote(partial.at[1], grams.at[me], gram_send.at[d], gram_recv.at[me], place(1, spot + d))
             copy.start()
             sends.append(copy)
+        upper.start()
         for d in range(1, n_plane):
             source = (spot + d) % n_plane
             remote(partial.at[0], early.at[source], early_send.at[d], early_recv.at[source], place(0, source)).wait_recv()

time: 24.9 us -> 24.3 us (0.976); the launches traced: 24.5 us -> 24.2 us
  Pallas kernels: 22.4 us -> 22.1 us
    pallas_call x1, Pallas kernels: 22.4 us -> 22.1 us  [fused_body(): pl.pallas_call(functools.partial(kernel, sizes), out_shape=pltpu.VMEM(blo...]
where the time goes in v8:
time: 24.3 us; the launch traced here: 24.2 us
  Pallas kernels  22.1 us (91%)
  between operations  1.3 us (5%)
  local copies, waits for them, and re-layouts  0.8 us (3%)
    pallas_call x1, Pallas kernels, fused_body(): pl.pallas_call(functools.partial(kernel, sizes), out_shape=pltpu.VMEM(blo...  22.1 us
    unnamed x1, local copies, waits for them, and re-layouts  0.8 us

profile of v8, /device:TPU:2, one launch (start us, length us, event | category | flops | bytes accessed | tf_op | source)
XLA Modules:
  0.0 24.2 jit_solution(2307072939845366539)
XLA Ops:
  1.3 22.1 %shard_map.55 = f32[4,64,512]{2,1,0:T(8,128)S(1)} custom-call(f32[4,64,512]{2,1,0:T(8,128)} %vec_hbm.1, s32[64,512]{1,0:T(8,128)} %lev_hbm.1, f32[8]{0:T(128)} %table_hbm.1, f32[1]{0:T(128)S(6)} %copy.8.low_ref, f32[1]{0:T(128)S(6)} %copy.9.high_ref), custom_call_target="tpu_custom_call" | custom-call | tf_op jit(solution)/shard_map/pallas_call | solution.py:471
  23.4 0.8 %copy.7 = f32[4,64,512]{2,1,0:T(8,128)} copy(f32[4,64,512]{2,1,0:T(8,128)S(1)} %shard_map.55) | data formatting | bytes 1048576
